TPU v7x, 256 devices: a whole 4x4x8 slice. The times are simulated.
256 devices in a mesh: row: 32 (over z_lo, y, x), col: 8 (over z_hi, core).
Axes of the slice: x: 4, y: 4, z: 8 (z_hi: 4, z_lo: 2; z = z_hi * 2 + z_lo), core: 2. Of those that a mesh axis runs over, the one named last changes fastest.
Arguments:
- features: bfloat16 [512, 512, 1024], P('row', None, 'col'), may hold values from -6 to 6
- projection: bfloat16 [512, 4], replicated, may hold values from -0.25 to 0.25
- norm_gain: bfloat16 [2048], replicated, may hold values from 0.25 to 1.75
- norm_shift: bfloat16 [2048], replicated, may hold values from -6 to 6
- weight_in: bfloat16 [2048, 4096], P(None, 'col'), may hold values from -0.125 to 0.125
- weight_out: bfloat16 [4096, 1, 1024], P('col'), may hold values from -0.09375 to 0.09375
- cotangent: bfloat16 [512, 1, 1024], P('row', None, 'col'), may hold values from -6 to 6
Outputs:
- mixed: bfloat16 [512, 1, 1024], P('row', None, 'col')
- grad_features: bfloat16 [512, 512, 1024], P('row', None, 'col')
- grad_gain: float32 [2048], replicated
- grad_shift: float32 [2048], replicated
- grad_weight_in: bfloat16 [2048, 4096], P(None, 'col')
- grad_weight_out: bfloat16 [4096, 1, 1024], P('col')
All inputs are finite; a program needn't handle non-finite values.
Results may differ from a plain program's by a relative error of at most 0.013.
Values may be sent and summed in bfloat16 or wider, within the bound.
A program may use at most 64 MiB of HBM per device.

v0:
```python
import jax
import jax.numpy as jnp
from jax import lax
from jax.sharding import PartitionSpec as P


def layer_norm(inter, norm_gain, norm_shift):
    mean = jnp.mean(inter, axis=1, keepdims=True)
    centered = inter - mean
    rstd = lax.rsqrt(jnp.mean(centered * centered, axis=1, keepdims=True) + 1e-05)
    unit = centered * rstd
    normed = (unit * norm_gain.astype(jnp.float32) + norm_shift.astype(jnp.float32)).astype(
        jnp.bfloat16
    )
    return (normed, unit, rstd)


def on_device(features, projection, norm_gain, norm_shift, weight_in, weight_out, cotangent):
    batch = features.shape[0]
    embeds = features.shape[1]
    reduced = jnp.einsum(
        "bnd,nk->bdk", features, projection, preferred_element_type=jnp.float32
    ).astype(jnp.bfloat16)
    partial_inter = jnp.einsum(
        "bnd,bdk->bnk", features, reduced, preferred_element_type=jnp.float32
    ).reshape(batch, -1)
    inter = lax.psum(partial_inter, "col")
    normed, unit, rstd = layer_norm(inter, norm_gain, norm_shift)
    pre = jnp.dot(normed, weight_in, preferred_element_type=jnp.float32)
    act = jax.nn.silu(pre).astype(jnp.bfloat16)
    out_terms = jnp.einsum("bh,hfd->bfd", act, weight_out, preferred_element_type=jnp.float32)
    mixed = lax.psum_scatter(out_terms, "col", scatter_dimension=2, tiled=True).astype(jnp.bfloat16)
    full_grads = lax.all_gather(cotangent, "col", axis=2, tiled=True)
    dact = jnp.einsum("bfd,hfd->bh", full_grads, weight_out, preferred_element_type=jnp.float32)
    sigma = jax.nn.sigmoid(pre)
    dpre = (dact * sigma * (1.0 + pre * (1.0 - sigma))).astype(jnp.bfloat16)
    partial_dnormed = jnp.einsum("bh,ih->bi", dpre, weight_in, preferred_element_type=jnp.float32)
    dnormed = lax.psum(partial_dnormed, "col")
    gain_terms = jnp.sum(dnormed * unit, axis=0)
    shift_terms = jnp.sum(dnormed, axis=0)
    in_terms = jnp.einsum("bi,bh->ih", normed, dpre, preferred_element_type=jnp.float32)
    out_grad_terms = jnp.einsum("bh,bfd->hfd", act, full_grads, preferred_element_type=jnp.float32)
    grad_in, grad_out, grad_gain, grad_shift = lax.psum(
        (in_terms, out_grad_terms, gain_terms, shift_terms), "row"
    )
    scaled = dnormed * norm_gain.astype(jnp.float32)
    dinter = rstd * (
        scaled
        - jnp.mean(scaled, axis=1, keepdims=True)
        - unit * jnp.mean(scaled * unit, axis=1, keepdims=True)
    )
    dinter = dinter.reshape(batch, embeds, -1)
    dreduced = jnp.einsum("bnd,bnk->bdk", features, dinter, preferred_element_type=jnp.float32)
    grad_features = jnp.einsum("bnk,bdk->bnd", dinter, reduced, preferred_element_type=jnp.float32)
    grad_features = grad_features + jnp.einsum(
        "nk,bdk->bnd", projection, dreduced, preferred_element_type=jnp.float32
    )
    return (
        mixed,
        grad_features.astype(jnp.bfloat16),
        grad_gain,
        grad_shift,
        grad_in.astype(jnp.bfloat16),
        grad_out.astype(jnp.bfloat16),
    )


def solution(mesh):
    placed = (
        P("row", None, "col"),
        P(),
        P(),
        P(),
        P(None, "col"),
        P("col", None, None),
        P("row", None, "col"),
    )
    return jax.shard_map(
        on_device,
        mesh=mesh,
        in_specs=placed,
        out_specs=(
            P("row", None, "col"),
            P("row", None, "col"),
            P(),
            P(),
            P(None, "col"),
            P("col", None, None),
        ),
        check_vma=False,
    )
```

profile of v0, /device:TPU:32, one launch (start us, length us, event | category | flops | bytes accessed | tf_op | source)
XLA Modules:
  0.0 379.2 jit_solution(18031466390064069782)
XLA Ops:
  7.2 0.0 copy-start
  7.2 0.0 all-reduce.5.cloned.1.call-start
  7.2 1.5 copy-done
  8.8 1.1 convolution_convert_fusion
  9.8 0.0 copy-start.5
  9.8 0.0 copy-start.6
  9.8 0.0 copy-start.7
  9.8 0.6 convolution_bitcast_fusion.1
  10.5 0.4 copy.15
  10.9 1.0 copy.16
  11.9 0.0 all-reduce.5.cloned.1.call-update
  11.9 0.0 all-reduce.7.cloned.1.call-start
  11.9 0.0 copy-done.5
  12.0 0.0 copy-done.6
  12.0 0.0 copy-done.7
  12.0 17.3 %all_gather.3 = bf16[16,1,1024]{2,0,1:T(8,128)(2,1)S(1)} all-gather(bf16[16,1,128]{2,0,1:T(8,128)(2,1)S(1)} %copy-done.7), channel_id=1, replica_groups=mesh['row'=32,'col'=8] {'col'}, dimensions={2}, use_global_device_ids=true | all-gather | bytes 36864 | tf_op jit(solution)/shard_map/all_gather | solution.py:33
  29.3 56.6 %all-reduce.5.cloned.1.call-done = f32[16,2048]{1,0:T(8,128)} async-done(((f32[16,2048]{1,0:T(8,128)}), f32[16,2048]{1,0:T(8,128)}) %all-reduce.5.cloned.1.call-update) | async-done | bytes 131088 | tf_op jit(solution)/shard_map/psum | solution.py:27
  85.8 1.0 reduce_sum.54
  86.9 1.1 multiply_reduce_fusion.2
  88.0 0.0 copy-start.3
  88.0 2.2 fusion.10
  90.2 0.0 copy-start.1
  90.2 1.9 convolution_bitcast_fusion
  92.0 0.0 copy-done.3
  92.0 0.0 copy-start.2
  92.0 0.4 fusion.2
  92.4 0.0 copy-done.1
  92.4 1.3 fusion.11
  93.8 0.0 all-reduce.7.cloned.1.call-update
  93.8 0.0 reduce-scatter.2.cloned.1.call-start
  93.8 0.0 copy-done.2
  93.8 2.7 fusion.9
  96.6 0.9 convolution_bitcast_fusion.2
  97.4 0.0 reduce-scatter.2.cloned.1.call-update
  97.5 66.6 %all-reduce.7.cloned.1.call-done = f32[16,2048]{1,0:T(8,128)} async-done(((f32[16,2048]{1,0:T(8,128)}), f32[16,2048]{1,0:T(8,128)}) %all-reduce.7.cloned.1.call-update) | async-done | bytes 131088 | tf_op jit(solution)/shard_map/psum | solution.py:38
  164.1 1.1 multiply_reduce_fusion
  165.2 1.0 subtract_multiply_fusion
  166.2 0.3 copy.17
  166.5 0.3 copy.18
  166.8 0.0 copy-start.4
  166.9 2.8 fusion.12
  169.6 0.0 copy-done.4
  169.6 4.5 %fusion = bf16[16,512,128]{2,1,0:T(8,128)(2,1)} fusion(f32[16,512,128]{2,1,0:T(8,128)} %fusion.12, bf16[16,512,4]{1,2,0:T(4,128)(2,1)S(1)} %copy.18, bf16[16,512,128]{2,1,0:T(8,128)(2,1)S(1)} %copy-done, bf16[512,4]{0,1:T(4,128)(2,1)S(1)} %copy-done.4), kind=kOutput, calls=%fused_computation.1 | convolution fusion | flops 18874368 | bytes 8458240 | tf_op jit(solution)/shard_map/nk,bdk->bnd/dot_general | solution.py:55
  174.1 197.3 %all-reduce.8 = (f32[2048]{0:T(1024)}, f32[2048]{0:T(1024)}, bf16[2048,512]{1,0:T(8,128)(2,1)}, bf16[512,1,1024]{2,0,1:T(8,128)(2,1)}) all-reduce(f32[2048]{0:T(1024)S(1)} %get-tuple-element.6, f32[2048]{0:T(1024)S(1)} %get-tuple-element.9, f32[2048,512]{1,0:T(8,128)} %fusion.9, ...), channel_id=1, replica_groups=mesh['row'=32,'col'=8] {'row'}, use_global_device_ids=true, to_apply=%region_8.9 | all-reduce | flops 1576960 | bytes 9469952 | tf_op jit(solution)/shard_map/psum | solution.py:43
  371.3 0.0 reduce-scatter.2.cloned.1.call-done
  371.3 1.3 convert_element_type.36
  (5 shorter events, 0.0 us)
Async XLA Ops:
  7.2 1.6 copy-start
  7.2 78.6 %all-reduce.5.cloned.1.call-start = ((), (), s32[]{:S(2)}) async-start(), calls=%async_computation.1 | async-start | bytes 262144 | tf_op jit(solution)/shard_map/psum | solution.py:27
  9.8 2.1 copy-start.5
  9.8 2.1 copy-start.6
  9.8 2.2 copy-start.7
  11.9 152.2 %all-reduce.7.cloned.1.call-start = ((), (), s32[]{:S(2)}) async-start(), calls=%async_computation.3 | async-start | bytes 262144 | tf_op jit(solution)/shard_map/psum | solution.py:38
  88.0 4.1 %copy-start.3 = (bf16[512,1,1024]{2,0,1:T(8,128)(2,1)S(1)}, bf16[512,1,1024]{2,0,1:T(8,128)(2,1)}, u32[]{:S(2)}) copy-start(bf16[512,1,1024]{2,0,1:T(8,128)(2,1)} %param.12) | copy-start | bytes 3145732
  90.2 2.3 copy-start.1
  92.0 1.8 copy-start.2
  93.8 277.6 %reduce-scatter.2.cloned.1.call-start = ((), (), s32[]{:S(2)}) async-start(), calls=%async_computation.2 | async-start | bytes 73728 | tf_op jit(solution)/shard_map/reduce_scatter | solution.py:32
  166.8 2.8 copy-start.4
Sparse Core Ops, SparseCore 0:
  12.0 73.7 all-reduce.4
  93.9 70.1 all-reduce.6
  166.6 35.4 reduce-scatter.1
where the time goes:
time: 380 us; the launch traced here: 379 us
  blocking collectives  215 us (57%)
  waiting for transfers between devices  123 us (32%)
  matrix products  18.3 us (5%)
  between operations  13.9 us (4%)
  other arithmetic  5.58 us (1%)
    psum x1, blocking collectives, on_device(): lax.psum((in_terms, out_grad_terms, gain_terms, shift_terms), 'row')  197 us
    psum x1, waiting for transfers between devices, on_device(): dnormed = lax.psum(partial_dnormed, 'col')  66.6 us
    psum x1, waiting for transfers between devices, on_device(): inter = lax.psum(partial_inter, 'col')  56.6 us
    all_gather x1, blocking collectives, on_device(): full_grads = lax.all_gather(cotangent, 'col', axis=2, tiled=True)  17.3 us
  transfers between devices with their start and end apart: 3, of which 2 were waited for; matrix products, arithmetic and copies ran while one was open for 4% of the time, Pallas kernels for 0%

commit v1 on v0

v1 whole, which is shorter than its diff:
```python
import functools

import jax
import jax.numpy as jnp
from jax import lax
from jax.experimental import pallas as pl
from jax.experimental.pallas import tpu as pltpu
from jax.sharding import PartitionSpec as P

MESH = pl.DeviceIdType.MESH
F32 = jnp.float32
BF16 = jnp.bfloat16
NT = (((1,), (1,)), ((), ()))


class Links:
    def __init__(self, send_sems, recv_sems):
        self.send_sems = send_sems
        self.recv_sems = recv_sems
        self.count = 0
        self.sends = []

    def start(self, src, dst, land, row, col):
        i = self.count
        self.count += 1
        copy = pltpu.make_async_remote_copy(
            src_ref=src,
            dst_ref=dst,
            send_sem=self.send_sems.at[i],
            recv_sem=self.recv_sems.at[i],
            device_id={"row": row, "col": col},
            device_id_type=MESH,
        )
        copy.start()
        self.sends.append(copy)
        return pltpu.make_async_remote_copy(
            src_ref=land,
            dst_ref=land,
            send_sem=self.send_sems.at[i],
            recv_sem=self.recv_sems.at[i],
            device_id={"row": row, "col": col},
            device_id_type=MESH,
        )


class Gather:
    def __init__(self, links, buf, where):
        self.links = links
        self.buf = buf
        self.x, self.y, self.zl, self.core, self.row, self.col = where
        core = self.core
        self.f = (1 - core) * self.x + core * self.y
        self.s = (1 - core) * self.y + core * self.x
        self.first = {}
        self.second = {}
        self.relay_first = []
        self.relay_second = {}
        self.sibling = []

    def pos(self, core, df, ds):
        f = (1 - core) * self.x + core * self.y
        s = (1 - core) * self.y + core * self.x
        f = lax.rem(f + df + 4, 4)
        s = lax.rem(s + ds + 4, 4)
        return (1 - core) * (s * 4 + f) + core * (f * 4 + s)

    def block(self, df, ds, zl=None, core=None):
        core = self.core if core is None else core
        p = self.pos(core, df, ds) * 32
        if zl is None:
            return self.buf.at[core, pl.ds(pl.multiple_of(p, 32), 32), :]
        return self.buf.at[core, pl.ds(pl.multiple_of(p + zl * 16, 16), 16), :]

    def row_of(self, df, ds):
        return self.zl * 16 + self.pos(self.core, df, ds)

    def start_z(self):
        mine = self.block(0, 0, self.zl)
        mate = (1 - self.zl) * 16 + self.pos(self.core, 0, 0)
        self.z = self.links.start(mine, mine, self.block(0, 0, 1 - self.zl), mate, self.col)

    def to_sibling(self, df, ds, zl=None):
        mine = self.block(df, ds, zl)
        other = 1 - self.core
        self.sibling.append(
            self.links.start(
                mine, mine, self.block(df, ds, zl, core=other), self.row, self.col + 1 - 2 * self.core
            )
        )

    def start_first(self):
        self.z.wait_recv()
        mine = self.block(0, 0)
        for d in (1, -1):
            self.first[d] = self.links.start(mine, mine, self.block(-d, 0), self.row_of(d, 0), self.col)
        self.start_second(0)
        self.to_sibling(0, 0, 1 - self.zl)

    def start_second(self, df):
        mine = self.block(df, 0)
        for d in (1, -1):
            self.second[df, d] = self.links.start(
                mine, mine, self.block(df, -d), self.row_of(0, d), self.col
            )

    def relay_firsts(self):
        for d in (1, -1):
            zl = (1 - d) // 2
            self.first[d].wait_recv()
            part = self.block(-d, 0, zl)
            self.relay_first.append(
                self.links.start(part, part, self.block(2, 0, zl), self.row_of(d, 0), self.col)
            )
        for d in (1, -1):
            self.start_second(-d)
        for d in (1, -1):
            self.to_sibling(-d, 0)

    def end_first(self):
        for copy in self.relay_first:
            copy.wait_recv()
        self.start_second(2)
        self.to_sibling(2, 0)

    def relay_seconds(self, df):
        self.relay_second[df] = []
        for d in (1, -1):
            zl = (1 - d) // 2
            self.second[df, d].wait_recv()
            part = self.block(df, -d, zl)
            self.relay_second[df].append(
                self.links.start(part, part, self.block(df, 2, zl), self.row_of(0, d), self.col)
            )
        for d in (1, -1):
            self.to_sibling(df, -d)

    def end_second(self, df):
        for copy in self.relay_second[df]:
            copy.wait_recv()
        self.to_sibling(df, 2)

    def end(self):
        for copy in self.sibling:
            copy.wait_recv()


def exchange(
    part_ref, cot_ref, gain_ref, shift_ref, win_ref, wout_ref,
    dinter_ref, mixed_ref, terms_ref, rows_ref, cots_ref,
    sums_ref, inter_ref, unit_ref, pieces_ref, got_ref, out_ref, got_out_ref, full_ref,
    sum_x_ref, sum_y_ref, sum_z_ref, sum_all_ref,
    send_sems, recv_sems, local_sem,
):
    row = lax.axis_index("row")
    col = lax.axis_index("col")
    x = lax.rem(row, 4)
    y = lax.rem(row // 4, 4)
    zl = row // 16
    core = lax.rem(col, 2)
    peers = [lax.rem(col + k, 8) for k in range(1, 8)]
    sources = [lax.rem(col + 8 - k, 8) for k in range(1, 8)]
    xs = [zl * 16 + y * 4 + lax.rem(x + k, 4) for k in range(1, 4)]
    ys = [zl * 16 + lax.rem(y + k, 4) * 4 + x for k in range(1, 4)]
    mate = (1 - zl) * 16 + y * 4 + x

    barrier = pltpu.get_barrier_semaphore()
    for peer in peers:
        pl.semaphore_signal(barrier, inc=1, device_id={"row": row, "col": peer}, device_id_type=MESH)
    for other in xs + ys + [mate]:
        pl.semaphore_signal(barrier, inc=1, device_id={"row": other, "col": col}, device_id_type=MESH)
    pl.semaphore_wait(barrier, 14)

    links = Links(send_sems, recv_sems)
    where = (x, y, zl, core, row, col)
    gather_n = Gather(links, rows_ref, where)
    gather_c = Gather(links, cots_ref, where)
    here = pl.ds(pl.multiple_of((y * 4 + x) * 32 + zl * 16, 16), 16)

    inters = [
        links.start(part_ref.at[peer], sums_ref.at[k], sums_ref.at[k], row, peer)
        for k, peer in enumerate(peers)
    ]

    def cot_place(c):
        return cots_ref.at[c // 4, here, pl.ds(pl.multiple_of(lax.rem(c, 4) * 128, 128), 128)]

    own = pltpu.make_async_copy(cot_ref, cot_place(col), local_sem)
    own.start()
    slices = [
        links.start(cot_ref, cot_place(col), cot_place(source), row, peer)
        for peer, source in zip(peers, sources)
    ]
    total = part_ref[col]
    for k, copy in enumerate(inters):
        copy.wait_recv()
        total = total + sums_ref[k]
    inter_ref[col] = total
    inters = [
        links.start(inter_ref.at[col], inter_ref.at[col], inter_ref.at[source], row, peer)
        for peer, source in zip(peers, sources)
    ]
    own.wait()
    for copy in slices:
        copy.wait_recv()
    gather_c.start_z()
    dact = jnp.zeros((16, 512), F32)
    for half in range(2):
        dact = dact + lax.dot_general(
            cots_ref[half, here, :],
            wout_ref[:, half * 512 : (half + 1) * 512],
            NT,
            preferred_element_type=F32,
        )
    for copy in inters:
        copy.wait_recv()

    total = inter_ref[0]
    for j in range(1, 8):
        total = total + inter_ref[j]
    mean = jnp.sum(total, axis=1, keepdims=True) * (1.0 / 2048)
    square = jnp.zeros((16, 256), F32)
    for j in range(8):
        centered = inter_ref[j] - mean
        square = square + centered * centered
    rstd = lax.rsqrt(jnp.sum(square, axis=1, keepdims=True) * (1.0 / 2048) + 1e-05)
    pre = jnp.zeros((16, 512), F32)
    normed = []
    for j in range(8):
        at = slice(j * 256, (j + 1) * 256)
        unit = (inter_ref[j] - mean) * rstd
        unit_ref[j] = unit
        normed.append(
            (unit * gain_ref[:, at].astype(F32) + shift_ref[:, at].astype(F32)).astype(BF16)
        )
        rows_ref[j // 4, here, (j % 4) * 256 : (j % 4 + 1) * 256] = normed[j]
    gather_n.start_z()
    gather_c.start_first()
    for j in range(8):
        at = slice(j * 256, (j + 1) * 256)
        pre = pre + jnp.dot(normed[j], win_ref[at, :], preferred_element_type=F32)
    sigma = 1.0 / (1.0 + jnp.exp(-pre))
    act = (pre * sigma).astype(BF16)
    dpre = (dact * sigma * (1.0 + pre * (1.0 - sigma))).astype(BF16)
    for j in range(8):
        at = slice(j * 256, (j + 1) * 256)
        pieces_ref[j] = lax.dot_general(dpre, win_ref[at, :], NT, preferred_element_type=F32)
    dnormeds = [
        links.start(pieces_ref.at[peer], got_ref.at[k], got_ref.at[k], row, peer)
        for k, peer in enumerate(peers)
    ]
    gather_n.start_first()
    for j in range(8):
        out_ref[j] = jnp.dot(
            act, wout_ref[:, j * 128 : (j + 1) * 128], preferred_element_type=F32
        )
    outs = [
        links.start(out_ref.at[peer], got_out_ref.at[k], got_out_ref.at[k], row, peer)
        for k, peer in enumerate(peers)
    ]
    gather_c.relay_firsts()

    dnormed = pieces_ref[col]
    for k, copy in enumerate(dnormeds):
        copy.wait_recv()
        dnormed = dnormed + got_ref[k]
    full_ref[col] = dnormed
    dnormeds = [
        links.start(full_ref.at[col], full_ref.at[col], full_ref.at[source], row, peer)
        for peer, source in zip(peers, sources)
    ]
    gain_terms = jnp.sum(dnormed * unit_ref[col], axis=0, keepdims=True)
    shift_terms = jnp.sum(dnormed, axis=0, keepdims=True)
    sum_x_ref[x] = jnp.concatenate([gain_terms, shift_terms, jnp.zeros((6, 256), F32)], axis=0)
    sums = [
        links.start(sum_x_ref.at[x], sum_x_ref.at[x], sum_x_ref.at[lax.rem(x + 4 - k, 4)], xs[k - 1], col)
        for k in range(1, 4)
    ]
    gather_n.relay_firsts()
    gather_c.end_first()

    for copy in dnormeds:
        copy.wait_recv()
    first = jnp.zeros((16, 256), F32)
    second = jnp.zeros((16, 256), F32)
    for j in range(8):
        at = slice(j * 256, (j + 1) * 256)
        scaled = full_ref[j] * gain_ref[:, at].astype(F32)
        first = first + scaled
        second = second + scaled * unit_ref[j]
    first = jnp.sum(first, axis=1, keepdims=True) * (1.0 / 2048)
    second = jnp.sum(second, axis=1, keepdims=True) * (1.0 / 2048)
    for j in range(8):
        at = slice(j * 256, (j + 1) * 256)
        scaled = full_ref[j] * gain_ref[:, at].astype(F32)
        dinter_ref[:, at] = rstd * (scaled - first - unit_ref[j] * second)

    gather_n.end_first()
    for copy in sums:
        copy.wait_recv()
    sum_y_ref[y] = (sum_x_ref[0] + sum_x_ref[1]) + (sum_x_ref[2] + sum_x_ref[3])
    sums = [
        links.start(sum_y_ref.at[y], sum_y_ref.at[y], sum_y_ref.at[lax.rem(y + 4 - k, 4)], ys[k - 1], col)
        for k in range(1, 4)
    ]
    mixed = out_ref[col]
    for k, copy in enumerate(outs):
        copy.wait_recv()
        mixed = mixed + got_out_ref[k]
    mixed_ref[...] = mixed.astype(BF16)

    order = (0, -1, 1, 2)
    for df in order:
        gather_c.relay_seconds(df)
    for copy in sums:
        copy.wait_recv()
    sum_z_ref[zl] = (sum_y_ref[0] + sum_y_ref[1]) + (sum_y_ref[2] + sum_y_ref[3])
    sums = [links.start(sum_z_ref.at[zl], sum_z_ref.at[zl], sum_z_ref.at[1 - zl], mate, col)]
    for df in order[:2]:
        gather_n.relay_seconds(df)
    for df in order:
        gather_c.end_second(df)
    for copy in sums:
        copy.wait_recv()
    sum_all_ref[col] = sum_z_ref[0] + sum_z_ref[1]
    sums = [
        links.start(sum_all_ref.at[col], sum_all_ref.at[col], sum_all_ref.at[source], row, peer)
        for peer, source in zip(peers, sources)
    ]
    for df in order[2:]:
        gather_n.relay_seconds(df)
    for df in order:
        gather_n.end_second(df)
    for copy in sums:
        copy.wait_recv()
    for j in range(8):
        terms_ref[:, j * 256 : (j + 1) * 256] = sum_all_ref[j]
    gather_c.end()
    gather_n.end()
    for copy in links.sends:
        copy.wait_send()


def exchanged(part, cot, gain, shift, weight_in, weight_out):
    copies = 56 + 2 * 37
    vmem = pl.BlockSpec(memory_space=pltpu.VMEM)
    return pl.pallas_call(
        exchange,
        out_shape=(
            jax.ShapeDtypeStruct((16, 2048), F32),
            jax.ShapeDtypeStruct((16, 128), BF16),
            jax.ShapeDtypeStruct((8, 2048), F32),
            jax.ShapeDtypeStruct((2, 512, 1024), BF16),
            jax.ShapeDtypeStruct((2, 512, 512), BF16),
        ),
        in_specs=[vmem] * 6,
        out_specs=(vmem,) * 5,
        scratch_shapes=[
            pltpu.VMEM((7, 16, 256), F32),
            pltpu.VMEM((8, 16, 256), F32),
            pltpu.VMEM((8, 16, 256), F32),
            pltpu.VMEM((8, 16, 256), F32),
            pltpu.VMEM((7, 16, 256), F32),
            pltpu.VMEM((8, 16, 128), F32),
            pltpu.VMEM((7, 16, 128), F32),
            pltpu.VMEM((8, 16, 256), F32),
            pltpu.VMEM((4, 8, 256), F32),
            pltpu.VMEM((4, 8, 256), F32),
            pltpu.VMEM((2, 8, 256), F32),
            pltpu.VMEM((8, 8, 256), F32),
            pltpu.SemaphoreType.DMA((copies,)),
            pltpu.SemaphoreType.DMA((copies,)),
            pltpu.SemaphoreType.DMA,
        ],
        compiler_params=pltpu.CompilerParams(
            collective_id=0, has_side_effects=True, vmem_limit_bytes=40 * 1024 * 1024
        ),
    )(part, cot, gain, shift, weight_in, weight_out)


def on_device(features, projection, norm_gain, norm_shift, weight_in, weight_out, cotangent):
    batch = features.shape[0]
    embeds = features.shape[1]
    reduced = jnp.einsum(
        "bnd,nk->bdk", features, projection, preferred_element_type=F32
    ).astype(BF16)
    part = jnp.einsum("bnd,bdk->bnk", features, reduced, preferred_element_type=F32)
    part = part.reshape(batch, 8, 256).transpose(1, 0, 2)
    wide_out = weight_out.reshape(weight_out.shape[0], -1)
    dinter, mixed, terms, rows, cots = exchanged(
        part,
        cotangent.reshape(batch, -1),
        norm_gain.reshape(1, -1),
        norm_shift.reshape(1, -1),
        weight_in,
        wide_out,
    )
    dinter = dinter.reshape(batch, embeds, -1)
    dreduced = jnp.einsum("bnd,bnk->bdk", features, dinter, preferred_element_type=F32)
    grad_features = jnp.einsum("bnk,bdk->bnd", dinter, reduced, preferred_element_type=F32)
    grad_features = grad_features + jnp.einsum(
        "nk,bdk->bnd", projection, dreduced, preferred_element_type=F32
    )

    win = weight_in.reshape(2, 1024, -1)
    wout = wide_out.reshape(-1, 2, 512)
    pre = jnp.einsum("jri,jih->rh", rows, win, preferred_element_type=F32)
    dact = jnp.einsum("jrd,hjd->rh", cots, wout, preferred_element_type=F32)
    sigma = jax.nn.sigmoid(pre)
    act = (pre * sigma).astype(BF16)
    dpre = (dact * sigma * (1.0 + pre * (1.0 - sigma))).astype(BF16)
    grad_in = jnp.einsum("jri,rh->jih", rows, dpre, preferred_element_type=F32).astype(BF16)
    grad_out = jnp.einsum("rh,jrd->hjd", act, cots, preferred_element_type=F32).astype(BF16)
    return (
        mixed.reshape(batch, 1, -1),
        grad_features.astype(BF16),
        terms[0],
        terms[1],
        grad_in.reshape(weight_in.shape),
        grad_out.reshape(weight_out.shape),
    )


def solution(mesh):
    placed = (
        P("row", None, "col"),
        P(),
        P(),
        P(),
        P(None, "col"),
        P("col", None, None),
        P("row", None, "col"),
    )
    return jax.shard_map(
        on_device,
        mesh=mesh,
        in_specs=placed,
        out_specs=(
            P("row", None, "col"),
            P("row", None, "col"),
            P(),
            P(),
            P(None, "col"),
            P("col", None, None),
        ),
        check_vma=False,
    )
```

time: 380 us -> 85.2 us (0.22)
  the two profiles are of different devices: /device:TPU:32 before, /device:TPU:1 now
where the time goes in v1:
time: 85.2 us; the launch traced here: 84.4 us
  Pallas kernels  47.9 us (56%)
  matrix products  22 us (26%)
  local copies, waits for them, and re-layouts  13.7 us (16%)
    pallas_call x1, Pallas kernels, exchanged(): pl.pallas_call(exchange, out_shape=(jax.ShapeDtypeStruct((16, 2048), F32)...  47.9 us
    unnamed x18, local copies, waits for them, and re-layouts  6.82 us
    dot_general x1, matrix products, on_device(): jnp.einsum('jri,rh->jih', rows, dpre, preferred_element_type=F32)  5.51 us
    dot_general x1, matrix products, on_device(): pre = jnp.einsum('jri,jih->rh', rows, win, preferred_element_type=F32)  4.58 us
    dot_general x1, matrix products, on_device(): jnp.einsum('nk,bdk->bnd', projection, dreduced, preferred_element_type=F32)  4.47 us
    dot_general x1, matrix products, on_device(): jnp.einsum('rh,jrd->hjd', act, cots, preferred_element_type=F32)  3.04 us
    dot_general x1, matrix products, on_device(): jnp.einsum('bnk,bdk->bnd', dinter, reduced, preferred_element_type=F32)  2.73 us

profile of v1, /device:TPU:1, one launch (start us, length us, event | category | flops | bytes accessed | tf_op | source)
XLA Modules:
  0.0 84.4 jit_solution(18328677346414665596)
XLA Ops:
  0.6 0.0 copy-start
  0.6 0.8 reshape.44.gain_ref
  1.5 0.7 reshape.45.shift_ref
  2.2 0.1 copy-done
  2.2 1.1 %convolution_convert_fusion.2 = bf16[16,128,4]{1,2,0:T(4,128)(2,1)S(1)} fusion(bf16[16,512,128]{2,1,0:T(8,128)(2,1)S(1)} %copy-done, bf16[512,4]{0,1:T(4,128)(2,1)} %param.8), kind=kOutput, calls=%fused_computation.12 | convolution fusion | flops 8396800 | bytes 2117632 | tf_op jit(solution)/shard_map/bnd,nk->bdk/dot_general | solution.py:383
  3.3 0.0 copy-start.1
  3.3 0.6 convolution_bitcast_fusion.2
  4.0 0.0 copy-start.3
  4.0 1.3 %copy.18 = f32[16,512,4]{0,2,1:T(4,128)} copy(f32[16,512,4]{1,2,0:T(4,128)S(1)} %convolution_bitcast_fusion.2) | data formatting | bytes 262144 | tf_op jit(solution)/shard_map/bnd,bdk->bnk/dot_general | solution.py:386
  5.3 1.5 %copy.19 = f32[16,8,256]{2,0,1:T(8,128)S(1)} copy(f32[16,8,256]{0,2,1:T(8,128)} %bitcast.66) | data formatting | bytes 262144 | tf_op jit(solution)/shard_map/reshape | solution.py:387
  6.8 0.0 copy-done.1
  6.8 1.3 %copy.30 = bf16[512,1,1024]{0,2,1:T(8,128)(2,1)} copy(bf16[512,1,1024]{2,0,1:T(8,128)(2,1)S(1)} %copy-done.1) | data formatting | bytes 2097152 | tf_op jit(solution)/shard_map/reshape;reshape | solution.py:405
  8.1 0.0 copy-done.3
  8.1 0.0 copy-start.2
  8.1 1.6 %copy-done.2 = bf16[2048,512]{1,0:T(8,128)(2,1)S(1)} copy-done((bf16[2048,512]{1,0:T(8,128)(2,1)S(1)}, bf16[2048,512]{1,0:T(8,128)(2,1)}, u32[]{:S(2)}) %copy-start.2) | copy-done | bytes 2097176
  9.7 47.9 %shard_map.118 = (f32[16,2048]{1,0:T(8,128)S(1)}, bf16[16,128]{1,0:T(8,128)(2,1)S(1)}, f32[8,2048]{1,0:T(8,128)S(1)}, bf16[2,512,1024]{2,1,0:T(8,128)(2,1)S(1)}, bf16[2,512,512]{2,1,0:T(8,128)(2,1)S(1)}) custom-call(f32[8,16,256]{2,1,0:T(8,128)S(1)} %bitcast.63, bf16[16,128]{1,0:T(8,128)(2,1)S(1)} %bitcast.64, bf16[1,2048]{1,0:T(2,128)(2,1)S(1)} %reshape.44.gain_ref, ...), custom_call_target="tpu_custom_call" | custom-call | tf_op jit(solution)/shard_map/pallas_call | solution.py:346
  57.7 0.0 copy-start.4
  57.7 1.3 %copy-done.4 = bf16[2,512,1024]{2,1,0:T(8,128)(2,1)} copy-done((bf16[2,512,1024]{2,1,0:T(8,128)(2,1)}, bf16[2,512,1024]{2,1,0:T(8,128)(2,1)S(1)}, u32[]{:S(2)}) %copy-start.4) | copy-done | bytes 2097176
  59.0 0.0 copy-start.5
  59.0 1.0 %copy-done.5 = bf16[2,512,512]{2,1,0:T(8,128)(2,1)} copy-done((bf16[2,512,512]{2,1,0:T(8,128)(2,1)}, bf16[2,512,512]{2,1,0:T(8,128)(2,1)S(1)}, u32[]{:S(2)}) %copy-start.5) | copy-done | bytes 1048600
  59.9 0.6 fusion.11
  60.6 0.3 copy.20
  60.9 0.3 copy.21
  61.2 0.0 copy-start.6
  61.2 4.6 %convolution_bitcast_fusion = f32[512,512]{1,0:T(8,128)} fusion(bf16[2,512,1024]{2,1,0:T(8,128)(2,1)} %copy-done.4, bf16[2,1024,512]{2,1,0:T(8,128)(2,1)} %bitcast.62), kind=kOutput, calls=%fused_computation.4 | convolution fusion | flops 1073741824 | bytes 5242880 | tf_op jit(solution)/shard_map/jri,jih->rh/dot_general | solution.py:406
  65.8 0.0 copy-done.6
  65.8 5.5 %convolution_convert_fusion = bf16[2,1024,512]{2,1,0:T(8,128)(2,1)} fusion(bf16[2,512,1024]{2,1,0:T(8,128)(2,1)} %copy-done.4, bf16[2,512,512]{2,1,0:T(8,128)(2,1)S(1)} %copy-done.6, bf16[512,2,512]{0,2,1:T(8,128)(2,1)} %bitcast.68, f32[512,512]{1,0:T(8,128)} %convolution_bitcast_fusion), kind=kOutput, calls=%fused_computation.2 | convolution fusion | flops 1614020608 | bytes 7340032 | tf_op jit(solution)/shard_map/jri,rh->jih/dot_general | solution.py:411
  71.3 3.0 %convolution_convert_fusion.1 = bf16[512,2,512]{0,2,1:T(8,128)(2,1)} fusion(bf16[2,512,512]{2,1,0:T(8,128)(2,1)S(1)} %copy-done.6, f32[512,512]{1,0:T(8,128)} %convolution_bitcast_fusion), kind=kOutput, calls=%fused_computation.3 | convolution fusion | flops 538705920 | bytes 3145728 | tf_op jit(solution)/shard_map/rh,jrd->hjd/dot_general | solution.py:412
  74.3 2.3 %copy.25 = bf16[512,1,1024]{2,0,1:T(8,128)(2,1)} copy(bf16[512,1,1024]{0,2,1:T(8,128)(2,1)} %bitcast.69) | data formatting | bytes 2097152
  76.6 0.0 copy-start.7
  76.6 2.7 %fusion.12 = f32[16,512,128]{2,1,0:T(8,128)} fusion(bf16[16,512,4]{1,2,0:T(4,128)(2,1)S(1)} %copy.21, bf16[16,128,4]{1,2,0:T(4,128)(2,1)S(1)} %convolution_convert_fusion.2), kind=kOutput, calls=%fused_computation.22 | convolution fusion | flops 8388608 | bytes 4276224 | tf_op jit(solution)/shard_map/bnk,bdk->bnd/dot_general | solution.py:399
  79.3 0.0 copy-done.7
  79.3 4.5 %fusion = bf16[16,512,128]{2,1,0:T(8,128)(2,1)} fusion(f32[16,512,128]{2,1,0:T(8,128)} %fusion.12, bf16[16,512,4]{1,2,0:T(4,128)(2,1)S(1)} %copy.21, bf16[16,512,128]{2,1,0:T(8,128)(2,1)S(1)} %copy-done, bf16[512,4]{0,1:T(4,128)(2,1)S(1)} %copy-done.7), kind=kOutput, calls=%fused_computation.1 | convolution fusion | flops 18874368 | bytes 8458240 | tf_op jit(solution)/shard_map/nk,bdk->bnd/dot_general | solution.py:400
  83.8 0.6 copy.32
Async XLA Ops:
  0.6 1.6 %copy-start = (bf16[16,512,128]{2,1,0:T(8,128)(2,1)S(1)}, bf16[16,512,128]{2,1,0:T(8,128)(2,1)}, u32[]{:S(2)}) copy-start(bf16[16,512,128]{2,1,0:T(8,128)(2,1)} %param.7) | copy-start | bytes 6291460
  3.3 3.5 %copy-start.1 = (bf16[512,1,1024]{2,0,1:T(8,128)(2,1)S(1)}, bf16[512,1,1024]{2,0,1:T(8,128)(2,1)}, u32[]{:S(2)}) copy-start(bf16[512,1,1024]{2,0,1:T(8,128)(2,1)} %param.12) | copy-start | bytes 3145732
  4.0 4.2 %copy-start.3 = (bf16[16,1,128]{2,0,1:T(8,128)(2,1)S(1)}, bf16[16,1,128]{2,0,1:T(8,128)(2,1)}, u32[]{:S(2)}) copy-start(bf16[16,1,128]{2,0,1:T(8,128)(2,1)} %param.13) | copy-start | bytes 12292
  8.1 1.6 %copy-start.2 = (bf16[2048,512]{1,0:T(8,128)(2,1)S(1)}, bf16[2048,512]{1,0:T(8,128)(2,1)}, u32[]{:S(2)}) copy-start(bf16[2048,512]{1,0:T(8,128)(2,1)} %win_ref.1) | copy-start | bytes 6291460
  57.7 1.3 %copy-start.4 = (bf16[2,512,1024]{2,1,0:T(8,128)(2,1)}, bf16[2,512,1024]{2,1,0:T(8,128)(2,1)S(1)}, u32[]{:S(2)}) copy-start(bf16[2,512,1024]{2,1,0:T(8,128)(2,1)S(1)} %get-tuple-element.14) | copy-start | bytes 6291460
  59.0 1.0 %copy-start.5 = (bf16[2,512,512]{2,1,0:T(8,128)(2,1)}, bf16[2,512,512]{2,1,0:T(8,128)(2,1)S(1)}, u32[]{:S(2)}) copy-start(bf16[2,512,512]{2,1,0:T(8,128)(2,1)S(1)} %get-tuple-element.15) | copy-start | bytes 3145732
  61.2 4.6 %copy-start.6 = (bf16[2,512,512]{2,1,0:T(8,128)(2,1)S(1)}, bf16[2,512,512]{2,1,0:T(8,128)(2,1)}, u32[]{:S(2)}) copy-start(bf16[2,512,512]{2,1,0:T(8,128)(2,1)} %copy-done.5) | copy-start | bytes 3145732
  76.6 2.7 %copy-start.7 = (bf16[512,4]{0,1:T(4,128)(2,1)S(1)}, bf16[512,4]{0,1:T(4,128)(2,1)}, u32[]{:S(2)}) copy-start(bf16[512,4]{0,1:T(4,128)(2,1)} %param.8) | copy-start | bytes 12292

commit v2 on v0

v2 whole, which is shorter than its diff:
```python
import jax
import jax.numpy as jnp
from jax import lax
from jax.experimental import pallas as pl
from jax.experimental.pallas import tpu as pltpu
from jax.sharding import PartitionSpec as P

MESH = pl.DeviceIdType.MESH
F32 = jnp.float32
BF16 = jnp.bfloat16
NT = (((1,), (1,)), ((), ()))
TN = (((0,), (0,)), ((), ()))


def mm(a, b, dims=(((1,), (0,)), ((), ()))):
    return lax.dot_general(a, b, dims, preferred_element_type=F32)


class Links:
    def __init__(self, send_sems, recv_sems):
        self.send_sems = send_sems
        self.recv_sems = recv_sems
        self.count = 0
        self.sends = []

    def start(self, src, dst, land, row, col):
        i = self.count
        self.count += 1

        def copy(a, b):
            return pltpu.make_async_remote_copy(
                src_ref=a,
                dst_ref=b,
                send_sem=self.send_sems.at[i],
                recv_sem=self.recv_sems.at[i],
                device_id={"row": row, "col": col},
                device_id_type=MESH,
            )

        out = copy(src, dst)
        out.start()
        self.sends.append(out)
        return copy(land, land)


class Gather:
    def __init__(self, links, buf, where):
        self.links = links
        self.buf = buf
        self.x, self.y, self.zl, self.core, self.row, self.col = where
        self.first = {}
        self.second = {}
        self.sibling = []

    def pos(self, core, df, ds):
        f = (1 - core) * self.x + core * self.y
        s = (1 - core) * self.y + core * self.x
        f = lax.rem(f + df + 4, 4)
        s = lax.rem(s + ds + 4, 4)
        return (1 - core) * (s * 4 + f) + core * (f * 4 + s)

    def block(self, df, ds, zl=None, core=None):
        core = self.core if core is None else core
        p = self.pos(core, df, ds) * 32
        if zl is None:
            return self.buf.at[core, pl.ds(pl.multiple_of(p, 32), 32), :]
        return self.buf.at[core, pl.ds(pl.multiple_of(p + zl * 16, 16), 16), :]

    def start_first(self):
        mine = self.block(0, 0, self.zl)
        for df, other in ((0, 1), (1, 0), (-1, 0), (1, 1), (-1, 1), (2, 0), (2, 1)):
            zl = self.zl + other * (1 - 2 * self.zl)
            to = zl * 16 + self.pos(self.core, df, 0)
            self.first[df, other] = self.links.start(
                mine, mine, self.block(-df if df != 2 else 2, 0, zl), to, self.col
            )

    def to_sibling(self, df, ds, zl=None):
        mine = self.block(df, ds, zl)
        self.sibling.append(
            self.links.start(
                mine,
                mine,
                self.block(df, ds, zl, core=1 - self.core),
                self.row,
                self.col + 1 - 2 * self.core,
            )
        )

    def start_second(self, df):
        back = -df if df != 2 else 2
        for other in (0, 1):
            if (back, other) in self.first:
                self.first[back, other].wait_recv()
        mine = self.block(df, 0)
        for ds in (1, -1, 2):
            to = self.zl * 16 + self.pos(self.core, 0, ds)
            self.second[df, ds] = self.links.start(
                mine, mine, self.block(df, -ds if ds != 2 else 2), to, self.col
            )
        self.to_sibling(df, 0, None if df else 1 - self.zl)

    def end_second(self, df):
        for ds in (1, -1, 2):
            self.second[df, ds].wait_recv()
            self.to_sibling(df, -ds if ds != 2 else 2)

    def end(self):
        for copy in self.sibling:
            copy.wait_recv()


def rows_of(count, width):
    return lax.broadcasted_iota(jnp.int32, (count, width), 0)


def step(
    feat_hbm, proj_ref, gain_ref, shift_ref, win_hbm, wout_hbm, cot_ref,
    mixed_ref, gfeat_ref, gain_out_ref, shift_out_ref, gwin_ref, gwout_ref,
    feat_ref, win_ref, wout_ref, wink_ref, rows_ref, cots_ref, perm_ref,
    part_ref, half_ref, send_ref, got_ref, inter_ref, unit_ref,
    dpart_ref, dhalf_ref, dsend_ref, dgot_ref, dinter_ref,
    out_ref, got_out_ref, terms_ref, term_half_ref, term_z_ref, term_x_ref, term_y_ref, term_all_ref,
    act_ref, dpre_ref, dact_ref, send_sems, recv_sems, local_sems,
):
    row = lax.axis_index("row")
    col = lax.axis_index("col")
    x = lax.rem(row, 4)
    y = lax.rem(row // 4, 4)
    zl = row // 16
    core = lax.rem(col, 2)
    sibling = col + 1 - 2 * core
    mine = core * 4
    other = 4 - mine
    peers = [lax.rem(col + k, 8) for k in range(1, 8)]
    sources = [lax.rem(col + 8 - k, 8) for k in range(1, 8)]
    xs = [y * 4 + lax.rem(x + k, 4) for k in range(1, 4)]
    ys = [lax.rem(y + k, 4) * 4 + x for k in range(1, 4)]
    place = y * 4 + x
    mate = (1 - zl) * 16 + place

    barrier = pltpu.get_barrier_semaphore()

    def greet(to_row, to_col):
        pl.semaphore_signal(barrier, inc=1, device_id={"row": to_row, "col": to_col}, device_id_type=MESH)

    for peer in peers:
        greet(row, peer)
    for p in xs + ys:
        greet(zl * 16 + p, col)
    firsts = [(1 - core) * a + core * b for a, b in zip(xs, ys)]
    for p in firsts:
        greet((1 - zl) * 16 + p, col)
    greet(mate, col)
    for k in (1, 3, 5):
        greet(mate, peers[k])

    here = pl.ds(pl.multiple_of(place * 32 + zl * 16, 16), 16)

    def cot_place(c):
        return cots_ref.at[c // 4, here, pl.ds(pl.multiple_of(lax.rem(c, 4) * 128, 128), 128)]

    loads = [
        pltpu.make_async_copy(feat_hbm.at[pl.ds(4 * i, 4)], feat_ref.at[pl.ds(4 * i, 4)], local_sems.at[i])
        for i in range(4)
    ]
    loads.append(pltpu.make_async_copy(cot_ref, cot_place(col), local_sems.at[4]))
    loads.append(pltpu.make_async_copy(win_hbm, win_ref, local_sems.at[5]))
    loads.append(pltpu.make_async_copy(wout_hbm, wout_ref, local_sems.at[6]))
    for copy in loads:
        copy.start()

    batch = lax.rem(rows_of(64, 512), 16)
    batch_d = lax.rem(rows_of(64, 128), 16)
    pick = (rows_of(64, 4) // 16 == lax.broadcasted_iota(jnp.int32, (64, 4), 1)).astype(F32).astype(BF16)
    proj = mm(pick, proj_ref[...], NT)
    r = rows_of(512, 512)
    perm_ref[...] = (
        (lax.broadcasted_iota(jnp.int32, (512, 512), 1) == lax.rem(r, 128) * 4 + r // 128).astype(F32).astype(BF16)
    )

    def pair(q):
        return jnp.concatenate([feat_ref[2 * q], feat_ref[2 * q + 1]], axis=1)

    def by_features(left):
        total = jnp.zeros((64, 256), F32)
        for q in range(8):
            total = total + mm(jnp.where(batch // 2 == q, left, 0.0).astype(BF16), pair(q))
        return jnp.where(lax.rem(batch_d, 2) == 0, total[:, :128], total[:, 128:])

    def spread(value, q):
        return jnp.concatenate(
            [jnp.where(batch_d == 2 * q + i, value, 0.0) for i in range(2)], axis=1
        ).astype(BF16)

    for copy in loads[:4]:
        copy.wait()
    reduced = by_features(proj).astype(BF16).astype(F32)
    inter = jnp.zeros((64, 512), F32)
    for q in range(8):
        inter = inter + mm(spread(reduced, q), pair(q), NT)
    blocks = [inter[16 * (j // 2) : 16 * (j // 2) + 16, 256 * (j % 2) : 256 * (j % 2) + 256] for j in range(8)]
    total = blocks[0]
    for j in range(1, 8):
        total = total + blocks[j]
    mean = jnp.sum(total, axis=1, keepdims=True) * (1.0 / 2048)
    for j in range(8):
        part_ref[j] = blocks[j] - mean

    pl.semaphore_wait(barrier, 20)
    links = Links(send_sems, recv_sems)
    where = (x, y, zl, core, row, col)
    gather_n = Gather(links, rows_ref, where)
    gather_c = Gather(links, cots_ref, where)

    def fold(parts, landing, sending, landed):
        copy = links.start(parts.at[pl.ds(other, 4)], landing, landing, row, sibling)
        yield
        copy.wait_recv()
        for j in range(4):
            sending[j] = (parts[mine + j] + landing[j]).astype(BF16)
        copies = [links.start(sending, landed.at[k], landed.at[k], row, peers[2 * k + 1]) for k in range(3)]
        yield
        for copy in copies:
            copy.wait_recv()

    fold_inter = fold(part_ref, half_ref, send_ref, got_ref)
    next(fold_inter)
    loads[4].wait()
    slices = [
        links.start(cot_ref, cot_place(col), cot_place(source), row, peer)
        for peer, source in zip(peers, sources)
    ]
    next(fold_inter)

    loads[5].wait()
    for J in range(4):
        moved = mm(perm_ref[...], win_ref[512 * J : 512 * J + 512, :]).astype(BF16)
        for k in range(4):
            wink_ref[k * 512 + J * 128 : k * 512 + J * 128 + 128, :] = moved[k * 128 : k * 128 + 128, :]
    both = jnp.concatenate([gain_ref[...], shift_ref[...]], axis=0)
    moved = [mm(both[:, 512 * J : 512 * J + 512], perm_ref[...], NT) for J in range(4)]
    gains = []
    shifts = []
    for j in range(8):
        k, h = j // 2, j % 2
        wide = jnp.concatenate([moved[2 * h + i][:, 128 * k : 128 * k + 128] for i in range(2)], axis=1)
        gains.append(wide[0:1])
        shifts.append(wide[1:2])

    for copy in slices:
        copy.wait_recv()
    gather_c.start_first()
    loads[6].wait()
    dact = jnp.zeros((16, 512), F32)
    for half in range(2):
        dact = dact + mm(cots_ref[half, here, :], wout_ref[:, half * 512 : (half + 1) * 512], NT)

    next(fold_inter, None)
    for j in range(4):
        inter_ref[mine + j] = (send_ref[j].astype(F32) + got_ref[0, j].astype(F32)) + (
            got_ref[1, j].astype(F32) + got_ref[2, j].astype(F32)
        )
    half = inter_ref.at[pl.ds(mine, 4)]
    copy = links.start(half, half, inter_ref.at[pl.ds(other, 4)], row, sibling)
    copy.wait_recv()

    total = inter_ref[0]
    for j in range(1, 8):
        total = total + inter_ref[j]
    mean = jnp.sum(total, axis=1, keepdims=True) * (1.0 / 2048)
    square = jnp.zeros((16, 256), F32)
    for j in range(8):
        centered = inter_ref[j] - mean
        square = square + centered * centered
    rstd = lax.rsqrt(jnp.sum(square, axis=1, keepdims=True) * (1.0 / 2048) + 1e-05)
    normed = []
    for j in range(8):
        unit = (inter_ref[j] - mean) * rstd
        unit_ref[j] = unit
        normed.append((unit * gains[j] + shifts[j]).astype(BF16))
    stacked = jnp.concatenate(
        [
            jnp.concatenate(
                [normed[2 * k + J // 2][:, 128 * (J % 2) : 128 * (J % 2) + 128] for k in range(4)], axis=1
            )
            for J in range(4)
        ],
        axis=0,
    )
    natural = mm(stacked, perm_ref[...]).astype(BF16)
    for J in range(4):
        rows_ref[J // 2, here, 512 * (J % 2) : 512 * (J % 2) + 512] = natural[16 * J : 16 * J + 16, :]
    gather_n.start_first()

    pre = jnp.zeros((16, 512), F32)
    for j in range(8):
        pre = pre + mm(normed[j], wink_ref[j * 256 : (j + 1) * 256, :])
    sigma = 1.0 / (1.0 + jnp.exp(-pre))
    act = (pre * sigma).astype(BF16)
    dpre = (dact * sigma * (1.0 + pre * (1.0 - sigma))).astype(BF16)
    first = jnp.zeros((16, 256), F32)
    second = jnp.zeros((16, 256), F32)
    gain_terms = []
    shift_terms = []
    scaled = []
    for j in range(8):
        dnormed = mm(dpre, wink_ref[j * 256 : (j + 1) * 256, :], NT)
        gain_terms.append(jnp.sum(dnormed * unit_ref[j], axis=0, keepdims=True))
        shift_terms.append(jnp.sum(dnormed, axis=0, keepdims=True))
        scaled.append(dnormed * gains[j])
        first = first + scaled[j]
        second = second + scaled[j] * unit_ref[j]
    first = jnp.sum(first, axis=1, keepdims=True) * (1.0 / 2048)
    second = jnp.sum(second, axis=1, keepdims=True) * (1.0 / 2048)
    for j in range(8):
        dpart_ref[j] = rstd * (scaled[j] - first - unit_ref[j] * second)
    fold_dinter = fold(dpart_ref, dhalf_ref, dsend_ref, dgot_ref)
    next(fold_dinter)
    for h in range(2):
        terms_ref[h] = jnp.concatenate(gain_terms[4 * h : 4 * h + 4] + shift_terms[4 * h : 4 * h + 4], axis=0)
    term = links.start(terms_ref.at[1 - core], term_half_ref, term_half_ref, row, sibling)
    next(fold_dinter)

    def z_of(r, c):
        return (c // 2) * 2 + r // 16

    term.wait_recv()
    at = z_of(row, col)
    term_z_ref[at] = terms_ref[core] + term_half_ref[...]
    terms = []
    for k in range(4):
        for r in (row, mate):
            if k or r is mate:
                to = lax.rem(col + 2 * k, 8)
                source = lax.rem(col + 8 - 2 * k, 8)
                terms.append(
                    links.start(term_z_ref.at[at], term_z_ref.at[at], term_z_ref.at[z_of(r, source)], r, to)
                )
    for j in range(8):
        out_ref[j] = mm(act, wout_ref[:, j * 128 : (j + 1) * 128])
    outs = [
        links.start(out_ref.at[peer], got_out_ref.at[k], got_out_ref.at[k], row, peer)
        for k, peer in enumerate(peers)
    ]
    order = (0, 1, -1, 2)
    for df in order:
        gather_c.start_second(df)
    for df in order:
        gather_n.start_second(df)
    for df in order:
        gather_c.end_second(df)

    next(fold_dinter, None)
    for j in range(4):
        dinter_ref[mine + j] = (
            (dsend_ref[j].astype(F32) + dgot_ref[0, j].astype(F32))
            + (dgot_ref[1, j].astype(F32) + dgot_ref[2, j].astype(F32))
        ).astype(BF16)
    half = dinter_ref.at[pl.ds(mine, 4)]
    copy = links.start(half, half, dinter_ref.at[pl.ds(other, 4)], row, sibling)
    for term in terms:
        term.wait_recv()
    total = term_z_ref[0]
    for k in range(1, 8):
        total = total + term_z_ref[k]
    term_x_ref[x] = total
    terms = [
        links.start(term_x_ref.at[x], term_x_ref.at[x], term_x_ref.at[lax.rem(x + 4 - k, 4)], zl * 16 + xs[k - 1], col)
        for k in range(1, 4)
    ]
    copy.wait_recv()
    dinter = jnp.concatenate(
        [jnp.concatenate([dinter_ref[2 * k], dinter_ref[2 * k + 1]], axis=1) for k in range(4)], axis=0
    ).astype(F32)
    dreduced = by_features(dinter)
    left = jnp.transpose(jnp.concatenate([dinter, proj], axis=0)).astype(BF16)
    for q in range(8):
        right = jnp.concatenate([spread(reduced, q), spread(dreduced, q)], axis=0)
        grad = mm(left, right).astype(BF16)
        gfeat_ref[2 * q] = grad[:, :128]
        gfeat_ref[2 * q + 1] = grad[:, 128:]

    for term in terms:
        term.wait_recv()
    term_y_ref[y] = (term_x_ref[0] + term_x_ref[1]) + (term_x_ref[2] + term_x_ref[3])
    terms = [
        links.start(term_y_ref.at[y], term_y_ref.at[y], term_y_ref.at[lax.rem(y + 4 - k, 4)], zl * 16 + ys[k - 1], col)
        for k in range(1, 4)
    ]
    mixed = out_ref[col]
    for k, copy in enumerate(outs):
        copy.wait_recv()
        mixed = mixed + got_out_ref[k]
    mixed_ref[...] = mixed.astype(BF16)

    for df in order:
        gather_n.end_second(df)
    gather_c.end()

    def dacts(i, carry):
        at = pl.ds(pl.multiple_of(i * 256, 256), 256)
        dact_ref[at, :] = mm(cots_ref[0, at, :], wout_ref[:, :512], NT) + mm(
            cots_ref[1, at, :], wout_ref[:, 512:], NT
        )
        return carry

    lax.fori_loop(0, 2, dacts, 0)
    for term in terms:
        term.wait_recv()
    term_all_ref[core] = (term_y_ref[0] + term_y_ref[1]) + (term_y_ref[2] + term_y_ref[3])
    term = links.start(term_all_ref.at[core], term_all_ref.at[core], term_all_ref.at[1 - core], row, sibling)
    gather_n.end()

    def hidden(i, carry):
        at = pl.ds(pl.multiple_of(i * 256, 256), 256)
        pre = mm(rows_ref[0, at, :], win_ref[:1024, :]) + mm(rows_ref[1, at, :], win_ref[1024:, :])
        sigma = 1.0 / (1.0 + jnp.exp(-pre))
        act_ref[at, :] = (pre * sigma).astype(BF16)
        dpre_ref[at, :] = (dact_ref[at, :] * sigma * (1.0 + pre * (1.0 - sigma))).astype(BF16)
        return carry

    lax.fori_loop(0, 2, hidden, 0)

    def grads_in(i, carry):
        at = pl.ds(pl.multiple_of(i * 256, 256), 256)
        columns = pl.ds(pl.multiple_of(lax.rem(i, 4) * 256, 256), 256)
        gwin_ref[at, :] = mm(rows_ref[i // 4, :, columns], dpre_ref[...], TN).astype(BF16)
        return carry

    lax.fori_loop(0, 8, grads_in, 0)
    for half in range(2):
        gwout_ref[:, half * 512 : (half + 1) * 512] = mm(act_ref[...], cots_ref[half], TN).astype(BF16)

    term.wait_recv()
    lines = []
    for J in range(4):
        for base in (0, 4):
            lines.append(
                jnp.concatenate(
                    [
                        term_all_ref[
                            k // 2,
                            base + 2 * (k % 2) + J // 2 : base + 2 * (k % 2) + J // 2 + 1,
                            128 * (J % 2) : 128 * (J % 2) + 128,
                        ]
                        for k in range(4)
                    ],
                    axis=1,
                )
            )
    rest = jnp.concatenate(lines, axis=0)
    total = jnp.zeros((8, 512), F32)
    for _ in range(3):
        piece = rest.astype(BF16)
        rest = rest - piece.astype(F32)
        total = total + mm(piece, perm_ref[...])
    for J in range(4):
        gain_out_ref[:, J * 512 : J * 512 + 512] = total[2 * J : 2 * J + 1, :]
        shift_out_ref[:, J * 512 : J * 512 + 512] = total[2 * J + 1 : 2 * J + 2, :]
    for copy in links.sends:
        copy.wait_send()


def on_device(features, projection, norm_gain, norm_shift, weight_in, weight_out, cotangent):
    copies = 130
    vmem = pl.BlockSpec(memory_space=pltpu.VMEM)
    hbm = pl.BlockSpec(memory_space=pl.ANY)
    mixed, gfeat, gain, shift, gwin, gwout = pl.pallas_call(
        step,
        out_shape=(
            jax.ShapeDtypeStruct((16, 128), BF16),
            jax.ShapeDtypeStruct((16, 512, 128), BF16),
            jax.ShapeDtypeStruct((1, 2048), F32),
            jax.ShapeDtypeStruct((1, 2048), F32),
            jax.ShapeDtypeStruct((2048, 512), BF16),
            jax.ShapeDtypeStruct((512, 1024), BF16),
        ),
        in_specs=[hbm, vmem, vmem, vmem, hbm, hbm, vmem],
        out_specs=(vmem,) * 6,
        scratch_shapes=[
            pltpu.VMEM((16, 512, 128), BF16),
            pltpu.VMEM((2048, 512), BF16),
            pltpu.VMEM((512, 1024), BF16),
            pltpu.VMEM((2048, 512), BF16),
            pltpu.VMEM((2, 512, 1024), BF16),
            pltpu.VMEM((2, 512, 512), BF16),
            pltpu.VMEM((512, 512), BF16),
            pltpu.VMEM((8, 16, 256), F32),
            pltpu.VMEM((4, 16, 256), F32),
            pltpu.VMEM((4, 16, 256), BF16),
            pltpu.VMEM((3, 4, 16, 256), BF16),
            pltpu.VMEM((8, 16, 256), F32),
            pltpu.VMEM((8, 16, 256), F32),
            pltpu.VMEM((8, 16, 256), F32),
            pltpu.VMEM((4, 16, 256), F32),
            pltpu.VMEM((4, 16, 256), BF16),
            pltpu.VMEM((3, 4, 16, 256), BF16),
            pltpu.VMEM((8, 16, 256), BF16),
            pltpu.VMEM((8, 16, 128), F32),
            pltpu.VMEM((7, 16, 128), F32),
            pltpu.VMEM((2, 8, 256), F32),
            pltpu.VMEM((8, 256), F32),
            pltpu.VMEM((8, 8, 256), F32),
            pltpu.VMEM((4, 8, 256), F32),
            pltpu.VMEM((4, 8, 256), F32),
            pltpu.VMEM((2, 8, 256), F32),
            pltpu.VMEM((512, 512), BF16),
            pltpu.VMEM((512, 512), BF16),
            pltpu.VMEM((512, 512), F32),
            pltpu.SemaphoreType.DMA((copies,)),
            pltpu.SemaphoreType.DMA((copies,)),
            pltpu.SemaphoreType.DMA((7,)),
        ],
        compiler_params=pltpu.CompilerParams(
            collective_id=0, has_side_effects=True, vmem_limit_bytes=48 * 1024 * 1024
        ),
    )(
        features,
        projection,
        norm_gain.reshape(1, -1),
        norm_shift.reshape(1, -1),
        weight_in,
        weight_out.reshape(weight_out.shape[0], -1),
        cotangent.reshape(cotangent.shape[0], -1),
    )
    return (
        mixed.reshape(cotangent.shape),
        gfeat,
        gain.reshape(-1),
        shift.reshape(-1),
        gwin,
        gwout.reshape(weight_out.shape),
    )


def solution(mesh):
    placed = (
        P("row", None, "col"),
        P(),
        P(),
        P(),
        P(None, "col"),
        P("col", None, None),
        P("row", None, "col"),
    )
    return jax.shard_map(
        on_device,
        mesh=mesh,
        in_specs=placed,
        out_specs=(
            P("row", None, "col"),
            P("row", None, "col"),
            P(),
            P(),
            P(None, "col"),
            P("col", None, None),
        ),
        check_vma=False,
    )
```

time: 380 us -> 57.3 us (0.15)
  the two profiles are of different devices: /device:TPU:32 before, /device:TPU:1 now
where the time goes in v2:
time: 57.3 us; the launch traced here: 57.1 us
  Pallas kernels  46.9 us (82%)
  local copies, waits for them, and re-layouts  9.56 us (17%)
  between operations  0.66 us (1%)
    pallas_call x1, Pallas kernels, on_device(): pl.pallas_call(step, out_shape=(jax.ShapeDtypeStruct((16, 128), BF16), ja...  46.9 us
    unnamed x13, local copies, waits for them, and re-layouts  8.17 us

profile of v2, /device:TPU:1, one launch (start us, length us, event | category | flops | bytes accessed | tf_op | source)
XLA Modules:
  0.0 57.1 jit_solution(5896004682639148809)
XLA Ops:
  0.6 0.7 %reshape.36.gain_ref = bf16[1,2048]{1,0:T(2,128)(2,1)S(1)} reshape(bf16[2048]{0:T(1024)(128)(2,1)} %param.9) | data formatting | bytes 8192 | tf_op jit(solution)/shard_map/reshape | solution.py:521
  1.3 0.7 %reshape.37.shift_ref = bf16[1,2048]{1,0:T(2,128)(2,1)S(1)} reshape(bf16[2048]{0:T(1024)(128)(2,1)} %param.10) | data formatting | bytes 8192 | tf_op jit(solution)/shard_map/reshape | solution.py:522
  2.0 0.9 %copy.13.proj_ref = bf16[512,4]{1,0:T(8,128)(2,1)S(1)} copy(bf16[512,4]{0,1:T(4,128)(2,1)} %param.8) | data formatting | bytes 8192 | tf_op args[1]
  2.9 0.0 copy-start
  2.9 1.2 %copy-done = bf16[512,1,1024]{2,0,1:T(8,128)(2,1)S(1)} copy-done((bf16[512,1,1024]{2,0,1:T(8,128)(2,1)S(1)}, bf16[512,1,1024]{2,0,1:T(8,128)(2,1)}, u32[]{:S(2)}) %copy-start) | copy-done | bytes 1048600
  4.1 0.0 copy-start.1
  4.1 0.7 %copy-done.1 = bf16[16,1,128]{2,0,1:T(8,128)(2,1)S(1)} copy-done((bf16[16,1,128]{2,0,1:T(8,128)(2,1)S(1)}, bf16[16,1,128]{2,0,1:T(8,128)(2,1)}, u32[]{:S(2)}) %copy-start.1) | copy-done | bytes 4120
  4.8 46.9 %shard_map.118 = (bf16[16,128]{1,0:T(8,128)(2,1)S(1)}, bf16[16,512,128]{2,1,0:T(8,128)(2,1)S(1)}, f32[1,2048]{1,0:T(1,128)S(1)}, f32[1,2048]{1,0:T(1,128)S(1)}, ...) custom-call(bf16[16,512,128]{2,1,0:T(8,128)(2,1)} %feat_hbm.1, bf16[512,4]{1,0:T(8,128)(2,1)S(1)} %copy.13.proj_ref, ...), custom_call_target="tpu_custom_call" | custom-call | tf_op jit(solution)/shard_map/pallas_call | solution.py:469
  51.7 0.6 %copy.20 = bf16[16,1,128]{2,0,1:T(8,128)(2,1)} copy(bf16[16,1,128]{2,0,1:T(8,128)(2,1)S(1)} %bitcast.11) | data formatting | bytes 8192
  52.3 0.0 copy-start.2
  52.3 1.3 %copy.21 = bf16[16,512,128]{2,1,0:T(8,128)(2,1)} copy(bf16[16,512,128]{2,1,0:T(8,128)(2,1)S(1)} %get-tuple-element.25) | data formatting | bytes 4194304
  53.6 0.6 %copy.22 = f32[2048]{0:T(1024)} copy(f32[2048]{0:T(1024)S(1)} %bitcast.9) | data formatting | bytes 16384
  54.2 0.6 %copy.23 = f32[2048]{0:T(1024)} copy(f32[2048]{0:T(1024)S(1)} %bitcast.8) | data formatting | bytes 16384
  54.8 0.0 copy-done.2
  54.8 1.3 %copy.24 = bf16[2048,512]{1,0:T(8,128)(2,1)} copy(bf16[2048,512]{1,0:T(8,128)(2,1)S(1)} %copy-done.2) | data formatting | bytes 4194304
  56.1 1.0 %copy.25 = bf16[512,1,1024]{2,0,1:T(8,128)(2,1)} copy(bf16[512,1,1024]{2,0,1:T(8,128)(2,1)S(1)} %bitcast.6) | data formatting | bytes 2097152
Async XLA Ops:
  2.9 1.2 %copy-start = (bf16[512,1,1024]{2,0,1:T(8,128)(2,1)S(1)}, bf16[512,1,1024]{2,0,1:T(8,128)(2,1)}, u32[]{:S(2)}) copy-start(bf16[512,1,1024]{2,0,1:T(8,128)(2,1)} %param.12) | copy-start | bytes 3145732
  4.1 0.7 %copy-start.1 = (bf16[16,1,128]{2,0,1:T(8,128)(2,1)S(1)}, bf16[16,1,128]{2,0,1:T(8,128)(2,1)}, u32[]{:S(2)}) copy-start(bf16[16,1,128]{2,0,1:T(8,128)(2,1)} %param.13) | copy-start | bytes 12292
  52.3 2.5 %copy-start.2 = (bf16[2048,512]{1,0:T(8,128)(2,1)S(1)}, bf16[2048,512]{1,0:T(8,128)(2,1)}, u32[]{:S(2)}) copy-start(bf16[2048,512]{1,0:T(8,128)(2,1)} %get-tuple-element.28) | copy-start | bytes 6291460

commit v3 on v2

--- a/solution.py
+++ b/solution.py
@@ -115,13 +115,14 @@
 
 
 def step(
-    feat_hbm, proj_ref, gain_ref, shift_ref, win_hbm, wout_hbm, cot_ref,
-    mixed_ref, gfeat_ref, gain_out_ref, shift_out_ref, gwin_ref, gwout_ref,
-    feat_ref, win_ref, wout_ref, wink_ref, rows_ref, cots_ref, perm_ref,
+    feat_hbm, proj_hbm, gain_hbm, shift_hbm, win_hbm, wout_hbm, cot_hbm,
+    mixed_ref, gfeat_hbm, gain_out_ref, shift_out_ref, gwin_hbm, gwout_hbm,
+    feat_ref, proj_ref, norm_ref, win_ref, wout_ref, wink_ref, rows_ref, cots_ref, perm_ref,
     part_ref, half_ref, send_ref, got_ref, inter_ref, unit_ref,
     dpart_ref, dhalf_ref, dsend_ref, dgot_ref, dinter_ref,
     out_ref, got_out_ref, terms_ref, term_half_ref, term_z_ref, term_x_ref, term_y_ref, term_all_ref,
-    act_ref, dpre_ref, dact_ref, send_sems, recv_sems, local_sems,
+    act_ref, dpre_ref, dact_ref, gfeat_ref, gwin_ref, gwout_ref,
+    send_sems, recv_sems, local_sems, store_sems,
 ):
     row = lax.axis_index("row")
     col = lax.axis_index("col")
@@ -144,6 +145,25 @@
     def greet(to_row, to_col):
         pl.semaphore_signal(barrier, inc=1, device_id={"row": to_row, "col": to_col}, device_id_type=MESH)
 
+    here = pl.ds(pl.multiple_of(place * 32 + zl * 16, 16), 16)
+
+    def cot_place(c):
+        return cots_ref.at[c // 4, here, pl.ds(pl.multiple_of(lax.rem(c, 4) * 128, 128), 128)]
+
+    loads = [
+        pltpu.make_async_copy(feat_hbm.at[pl.ds(4 * i, 4)], feat_ref.at[pl.ds(4 * i, 4)], local_sems.at[i])
+        for i in range(4)
+    ]
+    loads.append(pltpu.make_async_copy(cot_hbm, cot_place(col), local_sems.at[4]))
+    loads.append(pltpu.make_async_copy(win_hbm, win_ref, local_sems.at[5]))
+    loads.append(pltpu.make_async_copy(wout_hbm, wout_ref, local_sems.at[6]))
+    loads.append(pltpu.make_async_copy(gain_hbm, norm_ref.at[0], local_sems.at[7]))
+    loads.append(pltpu.make_async_copy(shift_hbm, norm_ref.at[1], local_sems.at[8]))
+    load_proj = pltpu.make_async_copy(proj_hbm, proj_ref, local_sems.at[9])
+    load_proj.start()
+    for copy in loads[:5]:
+        copy.start()
+
     for peer in peers:
         greet(row, peer)
     for p in xs + ys:
@@ -155,28 +175,14 @@
     for k in (1, 3, 5):
         greet(mate, peers[k])
 
-    here = pl.ds(pl.multiple_of(place * 32 + zl * 16, 16), 16)
-
-    def cot_place(c):
-        return cots_ref.at[c // 4, here, pl.ds(pl.multiple_of(lax.rem(c, 4) * 128, 128), 128)]
-
-    loads = [
-        pltpu.make_async_copy(feat_hbm.at[pl.ds(4 * i, 4)], feat_ref.at[pl.ds(4 * i, 4)], local_sems.at[i])
-        for i in range(4)
-    ]
-    loads.append(pltpu.make_async_copy(cot_ref, cot_place(col), local_sems.at[4]))
-    loads.append(pltpu.make_async_copy(win_hbm, win_ref, local_sems.at[5]))
-    loads.append(pltpu.make_async_copy(wout_hbm, wout_ref, local_sems.at[6]))
-    for copy in loads:
-        copy.start()
-
-    batch = lax.rem(rows_of(64, 512), 16)
-    batch_d = lax.rem(rows_of(64, 128), 16)
-    pick = (rows_of(64, 4) // 16 == lax.broadcasted_iota(jnp.int32, (64, 4), 1)).astype(F32).astype(BF16)
-    proj = mm(pick, proj_ref[...], NT)
+    batch = rows_of(64, 512) & 15
+    batch_d = rows_of(64, 128) & 15
+    pick = (rows_of(64, 4) >> 4 == lax.broadcasted_iota(jnp.int32, (64, 4), 1)).astype(F32).astype(BF16)
+    load_proj.wait()
+    proj = mm(pick, proj_ref[...])
     r = rows_of(512, 512)
     perm_ref[...] = (
-        (lax.broadcasted_iota(jnp.int32, (512, 512), 1) == lax.rem(r, 128) * 4 + r // 128).astype(F32).astype(BF16)
+        (lax.broadcasted_iota(jnp.int32, (512, 512), 1) == (r & 127) * 4 + (r >> 7)).astype(F32).astype(BF16)
     )
 
     def pair(q):
@@ -185,8 +191,8 @@
     def by_features(left):
         total = jnp.zeros((64, 256), F32)
         for q in range(8):
-            total = total + mm(jnp.where(batch // 2 == q, left, 0.0).astype(BF16), pair(q))
-        return jnp.where(lax.rem(batch_d, 2) == 0, total[:, :128], total[:, 128:])
+            total = total + mm(jnp.where(batch >> 1 == q, left, 0.0).astype(BF16), pair(q))
+        return jnp.where(batch_d & 1 == 0, total[:, :128], total[:, 128:])
 
     def spread(value, q):
         return jnp.concatenate(
@@ -195,6 +201,8 @@
 
     for copy in loads[:4]:
         copy.wait()
+    for copy in loads[5:]:
+        copy.start()
     reduced = by_features(proj).astype(BF16).astype(F32)
     inter = jnp.zeros((64, 512), F32)
     for q in range(8):
@@ -219,34 +227,46 @@
         copy.wait_recv()
         for j in range(4):
             sending[j] = (parts[mine + j] + landing[j]).astype(BF16)
-        copies = [links.start(sending, landed.at[k], landed.at[k], row, peers[2 * k + 1]) for k in range(3)]
+        copies = [links.start(sending, landed.at[k], landed.at[k], row, peers[2 * k + 1]) for k in (1, 0, 2)]
         yield
         for copy in copies:
             copy.wait_recv()
 
     fold_inter = fold(part_ref, half_ref, send_ref, got_ref)
     next(fold_inter)
+    next(fold_inter)
     loads[4].wait()
     slices = [
-        links.start(cot_ref, cot_place(col), cot_place(source), row, peer)
+        links.start(cot_place(col), cot_place(col), cot_place(source), row, peer)
         for peer, source in zip(peers, sources)
     ]
-    next(fold_inter)
 
     loads[5].wait()
     for J in range(4):
         moved = mm(perm_ref[...], win_ref[512 * J : 512 * J + 512, :]).astype(BF16)
         for k in range(4):
             wink_ref[k * 512 + J * 128 : k * 512 + J * 128 + 128, :] = moved[k * 128 : k * 128 + 128, :]
-    both = jnp.concatenate([gain_ref[...], shift_ref[...]], axis=0)
-    moved = [mm(both[:, 512 * J : 512 * J + 512], perm_ref[...], NT) for J in range(4)]
+    loads[7].wait()
+    loads[8].wait()
+    lines = jnp.concatenate([norm_ref[0], norm_ref[1]], axis=0)
+    take = (rows_of(8, 32) & 3) * 4 + (rows_of(8, 32) >> 2) * 16
+    both = jnp.concatenate(
+        [
+            mm((lax.broadcasted_iota(jnp.int32, (8, 32), 1) == take + i).astype(F32).astype(BF16), lines)
+            for i in range(4)
+        ],
+        axis=1,
+    ).astype(BF16)
+    moved = mm(both, perm_ref[...], NT)
     gains = []
     shifts = []
     for j in range(8):
         k, h = j // 2, j % 2
-        wide = jnp.concatenate([moved[2 * h + i][:, 128 * k : 128 * k + 128] for i in range(2)], axis=1)
-        gains.append(wide[0:1])
-        shifts.append(wide[1:2])
+        for base, into in ((0, gains), (4, shifts)):
+            J = base + 2 * h
+            into.append(
+                jnp.concatenate([moved[J + i : J + i + 1, 128 * k : 128 * k + 128] for i in range(2)], axis=1)
+            )
 
     for copy in slices:
         copy.wait_recv()
@@ -292,6 +312,7 @@
     for J in range(4):
         rows_ref[J // 2, here, 512 * (J % 2) : 512 * (J % 2) + 512] = natural[16 * J : 16 * J + 16, :]
     gather_n.start_first()
+    order = (0, 1, -1, 2)
 
     pre = jnp.zeros((16, 512), F32)
     for j in range(8):
@@ -339,26 +360,14 @@
                 )
     for j in range(8):
         out_ref[j] = mm(act, wout_ref[:, j * 128 : (j + 1) * 128])
+    for df in order:
+        gather_c.start_second(df)
     outs = [
         links.start(out_ref.at[peer], got_out_ref.at[k], got_out_ref.at[k], row, peer)
         for k, peer in enumerate(peers)
     ]
-    order = (0, 1, -1, 2)
-    for df in order:
-        gather_c.start_second(df)
     for df in order:
         gather_n.start_second(df)
-    for df in order:
-        gather_c.end_second(df)
-
-    next(fold_dinter, None)
-    for j in range(4):
-        dinter_ref[mine + j] = (
-            (dsend_ref[j].astype(F32) + dgot_ref[0, j].astype(F32))
-            + (dgot_ref[1, j].astype(F32) + dgot_ref[2, j].astype(F32))
-        ).astype(BF16)
-    half = dinter_ref.at[pl.ds(mine, 4)]
-    copy = links.start(half, half, dinter_ref.at[pl.ds(other, 4)], row, sibling)
     for term in terms:
         term.wait_recv()
     total = term_z_ref[0]
@@ -369,17 +378,45 @@
         links.start(term_x_ref.at[x], term_x_ref.at[x], term_x_ref.at[lax.rem(x + 4 - k, 4)], zl * 16 + xs[k - 1], col)
         for k in range(1, 4)
     ]
+    for df in order:
+        gather_c.end_second(df)
+
+    def dacts(i, carry):
+        at = pl.ds(pl.multiple_of(i * 256, 256), 256)
+        dact_ref[at, :] = mm(cots_ref[0, at, :], wout_ref[:, :512], NT) + mm(
+            cots_ref[1, at, :], wout_ref[:, 512:], NT
+        )
+        return carry
+
+    gather_c.end()
+    lax.fori_loop(0, 2, dacts, 0)
+    next(fold_dinter, None)
+    for j in range(4):
+        dinter_ref[mine + j] = (
+            (dsend_ref[j].astype(F32) + dgot_ref[0, j].astype(F32))
+            + (dgot_ref[1, j].astype(F32) + dgot_ref[2, j].astype(F32))
+        ).astype(BF16)
+    half = dinter_ref.at[pl.ds(mine, 4)]
+    copy = links.start(half, half, dinter_ref.at[pl.ds(other, 4)], row, sibling)
     copy.wait_recv()
     dinter = jnp.concatenate(
         [jnp.concatenate([dinter_ref[2 * k], dinter_ref[2 * k + 1]], axis=1) for k in range(4)], axis=0
     ).astype(F32)
     dreduced = by_features(dinter)
+    stores = []
     left = jnp.transpose(jnp.concatenate([dinter, proj], axis=0)).astype(BF16)
     for q in range(8):
         right = jnp.concatenate([spread(reduced, q), spread(dreduced, q)], axis=0)
         grad = mm(left, right).astype(BF16)
         gfeat_ref[2 * q] = grad[:, :128]
         gfeat_ref[2 * q + 1] = grad[:, 128:]
+        if q % 2:
+            part = pl.ds(2 * q - 2, 4)
+            stores.append(
+                pltpu.make_async_copy(gfeat_ref.at[part], gfeat_hbm.at[part], store_sems.at[8 + q // 2])
+            )
+            stores[-1].start()
+            gather_n.end_second(order[q // 2])
 
     for term in terms:
         term.wait_recv()
@@ -394,23 +431,8 @@
         mixed = mixed + got_out_ref[k]
     mixed_ref[...] = mixed.astype(BF16)
 
-    for df in order:
-        gather_n.end_second(df)
-    gather_c.end()
-
-    def dacts(i, carry):
-        at = pl.ds(pl.multiple_of(i * 256, 256), 256)
-        dact_ref[at, :] = mm(cots_ref[0, at, :], wout_ref[:, :512], NT) + mm(
-            cots_ref[1, at, :], wout_ref[:, 512:], NT
-        )
-        return carry
-
-    lax.fori_loop(0, 2, dacts, 0)
-    for term in terms:
-        term.wait_recv()
-    term_all_ref[core] = (term_y_ref[0] + term_y_ref[1]) + (term_y_ref[2] + term_y_ref[3])
-    term = links.start(term_all_ref.at[core], term_all_ref.at[core], term_all_ref.at[1 - core], row, sibling)
     gather_n.end()
+
 
     def hidden(i, carry):
         at = pl.ds(pl.multiple_of(i * 256, 256), 256)
@@ -421,16 +443,22 @@
         return carry
 
     lax.fori_loop(0, 2, hidden, 0)
+    for term in terms:
+        term.wait_recv()
+    term_all_ref[core] = (term_y_ref[0] + term_y_ref[1]) + (term_y_ref[2] + term_y_ref[3])
+    term = links.start(term_all_ref.at[core], term_all_ref.at[core], term_all_ref.at[1 - core], row, sibling)
 
     def grads_in(i, carry):
         at = pl.ds(pl.multiple_of(i * 256, 256), 256)
         columns = pl.ds(pl.multiple_of(lax.rem(i, 4) * 256, 256), 256)
         gwin_ref[at, :] = mm(rows_ref[i // 4, :, columns], dpre_ref[...], TN).astype(BF16)
+        pltpu.make_async_copy(gwin_ref.at[at, :], gwin_hbm.at[at, :], store_sems.at[i]).start()
         return carry
 
     lax.fori_loop(0, 8, grads_in, 0)
-    for half in range(2):
-        gwout_ref[:, half * 512 : (half + 1) * 512] = mm(act_ref[...], cots_ref[half], TN).astype(BF16)
+    for i in range(8):
+        at = pl.ds(i * 256, 256)
+        stores.append(pltpu.make_async_copy(gwin_ref.at[at, :], gwin_hbm.at[at, :], store_sems.at[i]))
 
     term.wait_recv()
     lines = []
@@ -458,15 +486,44 @@
     for J in range(4):
         gain_out_ref[:, J * 512 : J * 512 + 512] = total[2 * J : 2 * J + 1, :]
         shift_out_ref[:, J * 512 : J * 512 + 512] = total[2 * J + 1 : 2 * J + 2, :]
+    for half in range(2):
+        columns = slice(half * 512, (half + 1) * 512)
+        gwout_ref[:, columns] = mm(act_ref[...], cots_ref[half], TN).astype(BF16)
+        stores.append(
+            pltpu.make_async_copy(gwout_ref.at[:, columns], gwout_hbm.at[:, columns], store_sems.at[12 + half])
+        )
+        stores[-1].start()
     for copy in links.sends:
         copy.wait_send()
+    for copy in stores:
+        copy.wait()
+
+
+def store(*refs):
+    sources, targets, held = refs[:6], refs[6:12], refs[12:18]
+    loads, stores = [], []
+    for source, target, buf in zip(sources, targets, held):
+        rows = source.shape[0]
+        parts = 4 if rows * source.shape[-1] > 65536 or len(source.shape) == 3 else 1
+        for i in range(parts):
+            at = pl.ds(i * (rows // parts), rows // parts)
+            n = len(loads)
+            loads.append(pltpu.make_async_copy(source.at[at], buf.at[at], refs[18].at[n]))
+            stores.append(pltpu.make_async_copy(buf.at[at], target.at[at], refs[19].at[n]))
+    for copy in loads:
+        copy.start()
+    for load, save in zip(loads, stores):
+        load.wait()
+        save.start()
+    for save in stores:
+        save.wait()
 
 
 def on_device(features, projection, norm_gain, norm_shift, weight_in, weight_out, cotangent):
     copies = 130
     vmem = pl.BlockSpec(memory_space=pltpu.VMEM)
-    hbm = pl.BlockSpec(memory_space=pl.ANY)
-    mixed, gfeat, gain, shift, gwin, gwout = pl.pallas_call(
+    hbm = pl.BlockSpec(memory_space=pltpu.HBM)
+    results = pl.pallas_call(
         step,
         out_shape=(
             jax.ShapeDtypeStruct((16, 128), BF16),
@@ -476,10 +533,12 @@
             jax.ShapeDtypeStruct((2048, 512), BF16),
             jax.ShapeDtypeStruct((512, 1024), BF16),
         ),
-        in_specs=[hbm, vmem, vmem, vmem, hbm, hbm, vmem],
-        out_specs=(vmem,) * 6,
+        in_specs=[hbm] * 7,
+        out_specs=(vmem, hbm, vmem, vmem, hbm, hbm),
         scratch_shapes=[
             pltpu.VMEM((16, 512, 128), BF16),
+            pltpu.VMEM((4, 512), BF16),
+            pltpu.VMEM((2, 16, 128), BF16),
             pltpu.VMEM((2048, 512), BF16),
             pltpu.VMEM((512, 1024), BF16),
             pltpu.VMEM((2048, 512), BF16),
@@ -508,22 +567,35 @@
             pltpu.VMEM((512, 512), BF16),
             pltpu.VMEM((512, 512), BF16),
             pltpu.VMEM((512, 512), F32),
+            pltpu.VMEM((16, 512, 128), BF16),
+            pltpu.VMEM((2048, 512), BF16),
+            pltpu.VMEM((512, 1024), BF16),
             pltpu.SemaphoreType.DMA((copies,)),
             pltpu.SemaphoreType.DMA((copies,)),
-            pltpu.SemaphoreType.DMA((7,)),
+            pltpu.SemaphoreType.DMA((10,)),
+            pltpu.SemaphoreType.DMA((14,)),
         ],
         compiler_params=pltpu.CompilerParams(
-            collective_id=0, has_side_effects=True, vmem_limit_bytes=48 * 1024 * 1024
+            collective_id=0, has_side_effects=True, vmem_limit_bytes=58 * 1024 * 1024
         ),
     )(
         features,
-        projection,
-        norm_gain.reshape(1, -1),
-        norm_shift.reshape(1, -1),
+        projection.T,
+        norm_gain.reshape(16, 128),
+        norm_shift.reshape(16, 128),
         weight_in,
         weight_out.reshape(weight_out.shape[0], -1),
         cotangent.reshape(cotangent.shape[0], -1),
     )
+    mixed, gfeat, gain, shift, gwin, gwout = pl.pallas_call(
+        store,
+        out_shape=tuple(jax.ShapeDtypeStruct(a.shape, a.dtype) for a in results),
+        in_specs=[pl.BlockSpec(memory_space=pl.ANY)] * 6,
+        out_specs=(hbm,) * 6,
+        scratch_shapes=[pltpu.VMEM(a.shape, a.dtype) for a in results]
+        + [pltpu.SemaphoreType.DMA((15,)), pltpu.SemaphoreType.DMA((15,))],
+        compiler_params=pltpu.CompilerParams(vmem_limit_bytes=58 * 1024 * 1024),
+    )(*results)
     return (
         mixed.reshape(cotangent.shape),
         gfeat,

time: 57.3 us -> 53.3 us (0.930); the launches traced: 57.1 us -> 52.4 us
  local copies, waits for them, and re-layouts: 9.56 us -> 0 us
  Pallas kernels: 46.9 us -> 51.8 us
    unnamed x13 -> x0, local copies, waits for them, and re-layouts: 8.17 us -> none
    pallas_call x0 -> x1, Pallas kernels: none -> 4.83 us  [on_device(): pl.pallas_call(store, out_shape=tuple((jax.ShapeDtypeStruct(a.shape, a.dt...]
    reshape x2 -> x0, local copies, waits for them, and re-layouts: 1.39 us -> none  [the longest x1 0.69 us: on_device(): norm_gain.reshape(1, -1)]
where the time goes in v3:
time: 53.3 us; the launch traced here: 52.4 us
  Pallas kernels  51.8 us (97%)
  between operations  0.64 us (1%)
    pallas_call x1, Pallas kernels, on_device(): pl.pallas_call(step, out_shape=(jax.ShapeDtypeStruct((16, 128), BF16), ja...  47 us
    pallas_call x1, Pallas kernels, on_device(): pl.pallas_call(store, out_shape=tuple((jax.ShapeDtypeStruct(a.shape, a.dt...  4.83 us

profile of v3, /device:TPU:1, one launch (start us, length us, event | category | flops | bytes accessed | tf_op | source)
XLA Modules:
  0.0 52.4 jit_solution(14353577072149293578)
XLA Ops:
  0.6 47.0 %shard_map.118 = (bf16[16,128]{1,0:T(8,128)(2,1)}, bf16[16,512,128]{2,1,0:T(8,128)(2,1)}, f32[1,2048]{1,0:T(1,128)}, f32[1,2048]{1,0:T(1,128)}, bf16[2048,512]{1,0:T(8,128)(2,1)}, /*index=5*/bf16[512,1024]{1,0:T(8,128)(2,1)}) custom-call(bf16[16,512,128]{2,1,0:T(8,128)(2,1)} %feat_hbm.1, bf16[4,512]{1,0:T(4,128)(2,1)} %bitcast.10, bf16[16,128]{1,0:T(8,128)(2,1)} %bitcast.11, ...), custom_call_target="tpu_custom_call" | custom-call | tf_op jit(solution)/shard_map/pallas_call | solution.py:526
  47.6 4.8 %shard_map.119 = (bf16[16,128]{1,0:T(8,128)(2,1)}, bf16[16,512,128]{2,1,0:T(8,128)(2,1)}, f32[1,2048]{1,0:T(1,128)}, f32[1,2048]{1,0:T(1,128)}, bf16[2048,512]{1,0:T(8,128)(2,1)}, /*index=5*/bf16[512,1024]{1,0:T(8,128)(2,1)}) custom-call(bf16[16,128]{1,0:T(8,128)(2,1)} %get-tuple-element.18.refs_0_, bf16[16,512,128]{2,1,0:T(8,128)(2,1)} %get-tuple-element.19.refs_1_, ...), custom_call_target="tpu_custom_call" | custom-call | tf_op jit(solution)/shard_map/pallas_call | solution.py:590

commit v4 on v3

--- a/solution.py
+++ b/solution.py
@@ -42,6 +42,11 @@
         self.sends.append(out)
         return copy(land, land)
 
+    def flush(self):
+        for copy in self.sends:
+            copy.wait_send()
+        self.sends = []
+
 
 class Gather:
     def __init__(self, links, buf, where):
@@ -66,13 +71,23 @@
             return self.buf.at[core, pl.ds(pl.multiple_of(p, 32), 32), :]
         return self.buf.at[core, pl.ds(pl.multiple_of(p + zl * 16, 16), 16), :]
 
-    def start_first(self):
+    def start_first(self, diagonal):
         mine = self.block(0, 0, self.zl)
-        for df, other in ((0, 1), (1, 0), (-1, 0), (1, 1), (-1, 1), (2, 0), (2, 1)):
+        for df, other in ((0, 1), (1, 0), (-1, 0), (2, 0)) + (((1, 1), (-1, 1), (2, 1)) if diagonal else ()):
             zl = self.zl + other * (1 - 2 * self.zl)
             to = zl * 16 + self.pos(self.core, df, 0)
             self.first[df, other] = self.links.start(
                 mine, mine, self.block(-df if df != 2 else 2, 0, zl), to, self.col
+            )
+
+    def relay_mate(self):
+        self.first.pop((0, 1)).wait_recv()
+        zl = 1 - self.zl
+        mates = self.block(0, 0, zl)
+        for df in (1, -1, 2):
+            to = self.zl * 16 + self.pos(self.core, df, 0)
+            self.first[df, 1] = self.links.start(
+                mates, mates, self.block(-df if df != 2 else 2, 0, zl), to, self.col
             )
 
     def to_sibling(self, df, ds, zl=None):
@@ -91,7 +106,7 @@
         back = -df if df != 2 else 2
         for other in (0, 1):
             if (back, other) in self.first:
-                self.first[back, other].wait_recv()
+                self.first.pop((back, other)).wait_recv()
         mine = self.block(df, 0)
         for ds in (1, -1, 2):
             to = self.zl * 16 + self.pos(self.core, 0, ds)
@@ -116,12 +131,12 @@
 
 def step(
     feat_hbm, proj_hbm, gain_hbm, shift_hbm, win_hbm, wout_hbm, cot_hbm,
-    mixed_ref, gfeat_hbm, gain_out_ref, shift_out_ref, gwin_hbm, gwout_hbm,
+    mixed_hbm, gfeat_hbm, gain_out_hbm, shift_out_hbm, gwin_hbm, gwout_hbm,
     feat_ref, proj_ref, norm_ref, win_ref, wout_ref, wink_ref, rows_ref, cots_ref, perm_ref,
     part_ref, half_ref, send_ref, got_ref, inter_ref, unit_ref,
     dpart_ref, dhalf_ref, dsend_ref, dgot_ref, dinter_ref,
     out_ref, got_out_ref, terms_ref, term_half_ref, term_z_ref, term_x_ref, term_y_ref, term_all_ref,
-    act_ref, dpre_ref, dact_ref, gfeat_ref, gwin_ref, gwout_ref,
+    act_ref, dpre_ref, dact_ref, gfeat_ref, gwin_ref, gwout_ref, mixed_ref, gain_out_ref, shift_out_ref,
     send_sems, recv_sems, local_sems, store_sems,
 ):
     row = lax.axis_index("row")
@@ -270,7 +285,7 @@
 
     for copy in slices:
         copy.wait_recv()
-    gather_c.start_first()
+    gather_c.start_first(True)
     loads[6].wait()
     dact = jnp.zeros((16, 512), F32)
     for half in range(2):
@@ -311,7 +326,7 @@
     natural = mm(stacked, perm_ref[...]).astype(BF16)
     for J in range(4):
         rows_ref[J // 2, here, 512 * (J % 2) : 512 * (J % 2) + 512] = natural[16 * J : 16 * J + 16, :]
-    gather_n.start_first()
+    gather_n.start_first(False)
     order = (0, 1, -1, 2)
 
     pre = jnp.zeros((16, 512), F32)
@@ -358,14 +373,11 @@
                 terms.append(
                     links.start(term_z_ref.at[at], term_z_ref.at[at], term_z_ref.at[z_of(r, source)], r, to)
                 )
-    for j in range(8):
-        out_ref[j] = mm(act, wout_ref[:, j * 128 : (j + 1) * 128])
+    gather_n.relay_mate()
     for df in order:
         gather_c.start_second(df)
-    outs = [
-        links.start(out_ref.at[peer], got_out_ref.at[k], got_out_ref.at[k], row, peer)
-        for k, peer in enumerate(peers)
-    ]
+    for j in range(8):
+        out_ref[j] = mm(act, wout_ref[:, j * 128 : (j + 1) * 128])
     for df in order:
         gather_n.start_second(df)
     for term in terms:
@@ -378,18 +390,13 @@
         links.start(term_x_ref.at[x], term_x_ref.at[x], term_x_ref.at[lax.rem(x + 4 - k, 4)], zl * 16 + xs[k - 1], col)
         for k in range(1, 4)
     ]
+    outs = [
+        links.start(out_ref.at[peer], got_out_ref.at[k], got_out_ref.at[k], row, peer)
+        for k, peer in enumerate(peers)
+    ]
     for df in order:
         gather_c.end_second(df)
 
-    def dacts(i, carry):
-        at = pl.ds(pl.multiple_of(i * 256, 256), 256)
-        dact_ref[at, :] = mm(cots_ref[0, at, :], wout_ref[:, :512], NT) + mm(
-            cots_ref[1, at, :], wout_ref[:, 512:], NT
-        )
-        return carry
-
-    gather_c.end()
-    lax.fori_loop(0, 2, dacts, 0)
     next(fold_dinter, None)
     for j in range(4):
         dinter_ref[mine + j] = (
@@ -398,14 +405,32 @@
         ).astype(BF16)
     half = dinter_ref.at[pl.ds(mine, 4)]
     copy = links.start(half, half, dinter_ref.at[pl.ds(other, 4)], row, sibling)
+    def dacts(i, carry):
+        at = pl.ds(pl.multiple_of(i * 256, 256), 256)
+        dact_ref[at, :] = mm(cots_ref[0, at, :], wout_ref[:, :512], NT) + mm(
+            cots_ref[1, at, :], wout_ref[:, 512:], NT
+        )
+        return carry
+
+    gather_c.end()
+    lax.fori_loop(0, 2, dacts, 0)
     copy.wait_recv()
     dinter = jnp.concatenate(
         [jnp.concatenate([dinter_ref[2 * k], dinter_ref[2 * k + 1]], axis=1) for k in range(4)], axis=0
     ).astype(F32)
+    links.flush()
     dreduced = by_features(dinter)
     stores = []
     left = jnp.transpose(jnp.concatenate([dinter, proj], axis=0)).astype(BF16)
     for q in range(8):
+        if q == 2:
+            for term in terms:
+                term.wait_recv()
+            term_y_ref[y] = (term_x_ref[0] + term_x_ref[1]) + (term_x_ref[2] + term_x_ref[3])
+            terms = [
+                links.start(term_y_ref.at[y], term_y_ref.at[y], term_y_ref.at[lax.rem(y + 4 - k, 4)], zl * 16 + ys[k - 1], col)
+                for k in range(1, 4)
+            ]
         right = jnp.concatenate([spread(reduced, q), spread(dreduced, q)], axis=0)
         grad = mm(left, right).astype(BF16)
         gfeat_ref[2 * q] = grad[:, :128]
@@ -418,18 +443,13 @@
             stores[-1].start()
             gather_n.end_second(order[q // 2])
 
-    for term in terms:
-        term.wait_recv()
-    term_y_ref[y] = (term_x_ref[0] + term_x_ref[1]) + (term_x_ref[2] + term_x_ref[3])
-    terms = [
-        links.start(term_y_ref.at[y], term_y_ref.at[y], term_y_ref.at[lax.rem(y + 4 - k, 4)], zl * 16 + ys[k - 1], col)
-        for k in range(1, 4)
-    ]
     mixed = out_ref[col]
     for k, copy in enumerate(outs):
         copy.wait_recv()
         mixed = mixed + got_out_ref[k]
     mixed_ref[...] = mixed.astype(BF16)
+    stores.append(pltpu.make_async_copy(mixed_ref, mixed_hbm, store_sems.at[14]))
+    stores[-1].start()
 
     gather_n.end()
 
@@ -486,6 +506,10 @@
     for J in range(4):
         gain_out_ref[:, J * 512 : J * 512 + 512] = total[2 * J : 2 * J + 1, :]
         shift_out_ref[:, J * 512 : J * 512 + 512] = total[2 * J + 1 : 2 * J + 2, :]
+    stores.append(pltpu.make_async_copy(gain_out_ref, gain_out_hbm, store_sems.at[15]))
+    stores[-1].start()
+    stores.append(pltpu.make_async_copy(shift_out_ref, shift_out_hbm, store_sems.at[16]))
+    stores[-1].start()
     for half in range(2):
         columns = slice(half * 512, (half + 1) * 512)
         gwout_ref[:, columns] = mm(act_ref[...], cots_ref[half], TN).astype(BF16)
@@ -493,8 +517,7 @@
             pltpu.make_async_copy(gwout_ref.at[:, columns], gwout_hbm.at[:, columns], store_sems.at[12 + half])
         )
         stores[-1].start()
-    for copy in links.sends:
-        copy.wait_send()
+    links.flush()
     for copy in stores:
         copy.wait()
 
@@ -521,7 +544,6 @@
 
 def on_device(features, projection, norm_gain, norm_shift, weight_in, weight_out, cotangent):
     copies = 130
-    vmem = pl.BlockSpec(memory_space=pltpu.VMEM)
     hbm = pl.BlockSpec(memory_space=pltpu.HBM)
     results = pl.pallas_call(
         step,
@@ -534,7 +556,7 @@
             jax.ShapeDtypeStruct((512, 1024), BF16),
         ),
         in_specs=[hbm] * 7,
-        out_specs=(vmem, hbm, vmem, vmem, hbm, hbm),
+        out_specs=(hbm,) * 6,
         scratch_shapes=[
             pltpu.VMEM((16, 512, 128), BF16),
             pltpu.VMEM((4, 512), BF16),
@@ -570,10 +592,13 @@
             pltpu.VMEM((16, 512, 128), BF16),
             pltpu.VMEM((2048, 512), BF16),
             pltpu.VMEM((512, 1024), BF16),
+            pltpu.VMEM((16, 128), BF16),
+            pltpu.VMEM((1, 2048), F32),
+            pltpu.VMEM((1, 2048), F32),
             pltpu.SemaphoreType.DMA((copies,)),
             pltpu.SemaphoreType.DMA((copies,)),
             pltpu.SemaphoreType.DMA((10,)),
-            pltpu.SemaphoreType.DMA((14,)),
+            pltpu.SemaphoreType.DMA((17,)),
         ],
         compiler_params=pltpu.CompilerParams(
             collective_id=0, has_side_effects=True, vmem_limit_bytes=58 * 1024 * 1024

time: 53.3 us -> 52.1 us (0.977); the launches traced: 52.4 us -> 52 us
  no operation moved by 1% of the time
where the time goes in v4:
time: 52.1 us; the launch traced here: 52 us
  Pallas kernels  51.3 us (98%)
  between operations  0.64 us (1%)
    pallas_call x1, Pallas kernels, on_device(): pl.pallas_call(step, out_shape=(jax.ShapeDtypeStruct((16, 128), BF16), ja...  46.5 us
    pallas_call x1, Pallas kernels, on_device(): pl.pallas_call(store, out_shape=tuple((jax.ShapeDtypeStruct(a.shape, a.dt...  4.83 us

profile of v4, /device:TPU:1, one launch (start us, length us, event | category | flops | bytes accessed | tf_op | source)
XLA Modules:
  0.0 52.0 jit_solution(10947676775457922827)
XLA Ops:
  0.6 46.5 %shard_map.118 = (bf16[16,128]{1,0:T(8,128)(2,1)}, bf16[16,512,128]{2,1,0:T(8,128)(2,1)}, f32[1,2048]{1,0:T(1,128)}, f32[1,2048]{1,0:T(1,128)}, bf16[2048,512]{1,0:T(8,128)(2,1)}, /*index=5*/bf16[512,1024]{1,0:T(8,128)(2,1)}) custom-call(bf16[16,512,128]{2,1,0:T(8,128)(2,1)} %feat_hbm.1, bf16[4,512]{1,0:T(4,128)(2,1)} %bitcast.10, bf16[16,128]{1,0:T(8,128)(2,1)} %bitcast.11, ...), custom_call_target="tpu_custom_call" | custom-call | tf_op jit(solution)/shard_map/pallas_call | solution.py:548
  47.2 4.8 %shard_map.119 = (bf16[16,128]{1,0:T(8,128)(2,1)}, bf16[16,512,128]{2,1,0:T(8,128)(2,1)}, f32[1,2048]{1,0:T(1,128)}, f32[1,2048]{1,0:T(1,128)}, bf16[2048,512]{1,0:T(8,128)(2,1)}, /*index=5*/bf16[512,1024]{1,0:T(8,128)(2,1)}) custom-call(bf16[16,128]{1,0:T(8,128)(2,1)} %get-tuple-element.18.refs_0_, bf16[16,512,128]{2,1,0:T(8,128)(2,1)} %get-tuple-element.19.refs_1_, ...), custom_call_target="tpu_custom_call" | custom-call | tf_op jit(solution)/shard_map/pallas_call | solution.py:615

commit v5 on v4

--- a/solution.py
+++ b/solution.py
@@ -71,23 +71,13 @@
             return self.buf.at[core, pl.ds(pl.multiple_of(p, 32), 32), :]
         return self.buf.at[core, pl.ds(pl.multiple_of(p + zl * 16, 16), 16), :]
 
-    def start_first(self, diagonal):
+    def start_first(self):
         mine = self.block(0, 0, self.zl)
-        for df, other in ((0, 1), (1, 0), (-1, 0), (2, 0)) + (((1, 1), (-1, 1), (2, 1)) if diagonal else ()):
+        for df, other in ((0, 1), (1, 0), (-1, 0), (2, 0), (1, 1), (-1, 1), (2, 1)):
             zl = self.zl + other * (1 - 2 * self.zl)
             to = zl * 16 + self.pos(self.core, df, 0)
             self.first[df, other] = self.links.start(
                 mine, mine, self.block(-df if df != 2 else 2, 0, zl), to, self.col
-            )
-
-    def relay_mate(self):
-        self.first.pop((0, 1)).wait_recv()
-        zl = 1 - self.zl
-        mates = self.block(0, 0, zl)
-        for df in (1, -1, 2):
-            to = self.zl * 16 + self.pos(self.core, df, 0)
-            self.first[df, 1] = self.links.start(
-                mates, mates, self.block(-df if df != 2 else 2, 0, zl), to, self.col
             )
 
     def to_sibling(self, df, ds, zl=None):
@@ -285,7 +275,7 @@
 
     for copy in slices:
         copy.wait_recv()
-    gather_c.start_first(True)
+    gather_c.start_first()
     loads[6].wait()
     dact = jnp.zeros((16, 512), F32)
     for half in range(2):
@@ -326,7 +316,7 @@
     natural = mm(stacked, perm_ref[...]).astype(BF16)
     for J in range(4):
         rows_ref[J // 2, here, 512 * (J % 2) : 512 * (J % 2) + 512] = natural[16 * J : 16 * J + 16, :]
-    gather_n.start_first(False)
+    gather_n.start_first()
     order = (0, 1, -1, 2)
 
     pre = jnp.zeros((16, 512), F32)
@@ -353,6 +343,8 @@
         dpart_ref[j] = rstd * (scaled[j] - first - unit_ref[j] * second)
     fold_dinter = fold(dpart_ref, dhalf_ref, dsend_ref, dgot_ref)
     next(fold_dinter)
+    for df in order:
+        gather_c.start_second(df)
     for h in range(2):
         terms_ref[h] = jnp.concatenate(gain_terms[4 * h : 4 * h + 4] + shift_terms[4 * h : 4 * h + 4], axis=0)
     term = links.start(terms_ref.at[1 - core], term_half_ref, term_half_ref, row, sibling)
@@ -373,9 +365,6 @@
                 terms.append(
                     links.start(term_z_ref.at[at], term_z_ref.at[at], term_z_ref.at[z_of(r, source)], r, to)
                 )
-    gather_n.relay_mate()
-    for df in order:
-        gather_c.start_second(df)
     for j in range(8):
         out_ref[j] = mm(act, wout_ref[:, j * 128 : (j + 1) * 128])
     for df in order:
@@ -523,22 +512,14 @@
 
 
 def store(*refs):
-    sources, targets, held = refs[:6], refs[6:12], refs[12:18]
-    loads, stores = [], []
-    for source, target, buf in zip(sources, targets, held):
-        rows = source.shape[0]
-        parts = 4 if rows * source.shape[-1] > 65536 or len(source.shape) == 3 else 1
-        for i in range(parts):
-            at = pl.ds(i * (rows // parts), rows // parts)
-            n = len(loads)
-            loads.append(pltpu.make_async_copy(source.at[at], buf.at[at], refs[18].at[n]))
-            stores.append(pltpu.make_async_copy(buf.at[at], target.at[at], refs[19].at[n]))
+    loads = [pltpu.make_async_copy(refs[i], refs[12 + i], refs[18].at[i]) for i in range(6)]
+    saves = [pltpu.make_async_copy(refs[12 + i], refs[6 + i], refs[19].at[i]) for i in range(6)]
     for copy in loads:
         copy.start()
-    for load, save in zip(loads, stores):
+    for load, save in zip(loads, saves):
         load.wait()
         save.start()
-    for save in stores:
+    for save in saves:
         save.wait()
 
 
@@ -618,7 +599,7 @@
         in_specs=[pl.BlockSpec(memory_space=pl.ANY)] * 6,
         out_specs=(hbm,) * 6,
         scratch_shapes=[pltpu.VMEM(a.shape, a.dtype) for a in results]
-        + [pltpu.SemaphoreType.DMA((15,)), pltpu.SemaphoreType.DMA((15,))],
+        + [pltpu.SemaphoreType.DMA((6,)), pltpu.SemaphoreType.DMA((6,))],
         compiler_params=pltpu.CompilerParams(vmem_limit_bytes=58 * 1024 * 1024),
     )(*results)
     return (

time: 52.1 us -> 50.4 us (0.967)
  Pallas kernels: 51.3 us -> 49.6 us
    pallas_call x1, Pallas kernels: 46.5 us -> 45.5 us  [on_device(): pl.pallas_call(step, out_shape=(jax.ShapeDtypeStruct((16, 128), BF16), ja...]
    pallas_call x1, Pallas kernels: 4.83 us -> 4.06 us  [on_device(): pl.pallas_call(store, out_shape=tuple((jax.ShapeDtypeStruct(a.shape, a.dt...]
where the time goes in v5:
time: 50.4 us; the launch traced here: 50.2 us
  Pallas kernels  49.6 us (98%)
  between operations  0.64 us (1%)
    pallas_call x1, Pallas kernels, on_device(): pl.pallas_call(step, out_shape=(jax.ShapeDtypeStruct((16, 128), BF16), ja...  45.5 us
    pallas_call x1, Pallas kernels, on_device(): pl.pallas_call(store, out_shape=tuple((jax.ShapeDtypeStruct(a.shape, a.dt...  4.06 us

profile of v5, /device:TPU:1, one launch (start us, length us, event | category | flops | bytes accessed | tf_op | source)
XLA Modules:
  0.0 50.2 jit_solution(3118766075669214364)
XLA Ops:
  0.6 45.5 %shard_map.118 = (bf16[16,128]{1,0:T(8,128)(2,1)}, bf16[16,512,128]{2,1,0:T(8,128)(2,1)}, f32[1,2048]{1,0:T(1,128)}, f32[1,2048]{1,0:T(1,128)}, bf16[2048,512]{1,0:T(8,128)(2,1)}, /*index=5*/bf16[512,1024]{1,0:T(8,128)(2,1)}) custom-call(bf16[16,512,128]{2,1,0:T(8,128)(2,1)} %feat_hbm.1, bf16[4,512]{1,0:T(4,128)(2,1)} %bitcast.10, bf16[16,128]{1,0:T(8,128)(2,1)} %bitcast.11, ...), custom_call_target="tpu_custom_call" | custom-call | tf_op jit(solution)/shard_map/pallas_call | solution.py:529
  46.2 4.1 %shard_map.119 = (bf16[16,128]{1,0:T(8,128)(2,1)}, bf16[16,512,128]{2,1,0:T(8,128)(2,1)}, f32[1,2048]{1,0:T(1,128)}, f32[1,2048]{1,0:T(1,128)}, bf16[2048,512]{1,0:T(8,128)(2,1)}, /*index=5*/bf16[512,1024]{1,0:T(8,128)(2,1)}) custom-call(bf16[16,128]{1,0:T(8,128)(2,1)} %get-tuple-element.18.refs_0_, bf16[16,512,128]{2,1,0:T(8,128)(2,1)} %get-tuple-element.19.refs_1_, ...), custom_call_target="tpu_custom_call" | custom-call | tf_op jit(solution)/shard_map/pallas_call | solution.py:596

commit v6 on v5

--- a/solution.py
+++ b/solution.py
@@ -512,8 +512,8 @@
 
 
 def store(*refs):
-    loads = [pltpu.make_async_copy(refs[i], refs[12 + i], refs[18].at[i]) for i in range(6)]
-    saves = [pltpu.make_async_copy(refs[12 + i], refs[6 + i], refs[19].at[i]) for i in range(6)]
+    loads = [pltpu.make_async_copy(refs[i], refs[12 + i], refs[18].at[i]) for i in (1, 4, 5, 0, 2, 3)]
+    saves = [pltpu.make_async_copy(refs[12 + i], refs[6 + i], refs[19].at[i]) for i in (1, 4, 5, 0, 2, 3)]
     for copy in loads:
         copy.start()
     for load, save in zip(loads, saves):

time: 50.4 us -> 50.3 us (level)
  no operation moved by 1% of the time
where the time goes in v6:
time: 50.3 us; the launch traced here: 50.2 us
  Pallas kernels  49.6 us (99%)
  between operations  0.64 us (1%)
    pallas_call x1, Pallas kernels, on_device(): pl.pallas_call(step, out_shape=(jax.ShapeDtypeStruct((16, 128), BF16), ja...  45.5 us
    pallas_call x1, Pallas kernels, on_device(): pl.pallas_call(store, out_shape=tuple((jax.ShapeDtypeStruct(a.shape, a.dt...  4.05 us

profile of v6, /device:TPU:1, one launch (start us, length us, event | category | flops | bytes accessed | tf_op | source)
XLA Modules:
  0.0 50.2 jit_solution(18205273597839562597)
XLA Ops:
  0.6 45.5 %shard_map.118 = (bf16[16,128]{1,0:T(8,128)(2,1)}, bf16[16,512,128]{2,1,0:T(8,128)(2,1)}, f32[1,2048]{1,0:T(1,128)}, f32[1,2048]{1,0:T(1,128)}, bf16[2048,512]{1,0:T(8,128)(2,1)}, /*index=5*/bf16[512,1024]{1,0:T(8,128)(2,1)}) custom-call(bf16[16,512,128]{2,1,0:T(8,128)(2,1)} %feat_hbm.1, bf16[4,512]{1,0:T(4,128)(2,1)} %bitcast.10, bf16[16,128]{1,0:T(8,128)(2,1)} %bitcast.11, ...), custom_call_target="tpu_custom_call" | custom-call | tf_op jit(solution)/shard_map/pallas_call | solution.py:529
  46.2 4.1 %shard_map.119 = (bf16[16,128]{1,0:T(8,128)(2,1)}, bf16[16,512,128]{2,1,0:T(8,128)(2,1)}, f32[1,2048]{1,0:T(1,128)}, f32[1,2048]{1,0:T(1,128)}, bf16[2048,512]{1,0:T(8,128)(2,1)}, /*index=5*/bf16[512,1024]{1,0:T(8,128)(2,1)}) custom-call(bf16[16,128]{1,0:T(8,128)(2,1)} %get-tuple-element.18.refs_0_, bf16[16,512,128]{2,1,0:T(8,128)(2,1)} %get-tuple-element.19.refs_1_, ...), custom_call_target="tpu_custom_call" | custom-call | tf_op jit(solution)/shard_map/pallas_call | solution.py:596
